TPU v7x, 32 devices: a whole 2x2x4 slice. The times are simulated.
32 devices in a mesh: rep: 8 (over y, x, core), shard: 4 (over z).
Axes of the slice: x: 2, y: 2, z: 4, core: 2. Of those that a mesh axis runs over, the one named last changes fastest.
Arguments:
- tokens: bfloat16 [32768, 1024], P(('rep', 'shard')), may hold values from -6 to 6
- encoder: bfloat16 [4096, 1024], P(('rep', 'shard')), may hold values from -6 to 6
- cotangent: bfloat16 [32768, 1024], P(('rep', 'shard')), may hold values from -6 to 6
- lengths: int32 [32], replicated, may hold values from 1 to 1024, as said below
- encoder_lengths: int32 [32], replicated, may hold values from 32 to 128, as said below
- dealt_order: int32 [32], replicated, may hold values from 0 to 31, as said below
- attention_weights: float32 [1024, 8, 1024], P('shard')
- expand_weight: float32 [1024, 4096], P('shard'), may hold values from -0.1875 to 0.1875
- shrink_weight: float32 [4096, 1024], P('shard'), may hold values from -0.09375 to 0.09375
- small_params: float32 [17408], replicated
- attention_rows: float32 [8, 1024], P(None, 'shard'), may hold values from 32.768 to 26214.4
- attention_cols: float32 [8, 1024], replicated, may hold values from 327.68 to 3276.8
- expand_rows: float32 [1024], P('shard'), may hold values from 163.84 to 114688
- expand_cols: float32 [4096], replicated, may hold values from 1638.4 to 13107.2
- shrink_rows: float32 [4096], P('shard'), may hold values from 163.84 to 114688
- shrink_cols: float32 [1024], replicated, may hold values from 1638.4 to 13107.2
- small_moment: float32 [17408], replicated, may hold values from 6553.6 to 52428.8
Outputs:
- output: bfloat16 [32768, 1024], P(('rep', 'shard'))
- input_grad: bfloat16 [32768, 1024], P(('rep', 'shard'))
- encoder_grad: bfloat16 [4096, 1024], P(('rep', 'shard'))
- attention_grad: float32 [1024, 8, 1024], P('shard')
- expand_grad: float32 [1024, 4096], P('shard')
- shrink_grad: float32 [4096, 1024], P('shard')
- small_grad: float32 [17408], replicated
- attention_new: float32 [1024, 8, 1024], P('shard')
- expand_new: float32 [1024, 4096], P('shard')
- shrink_new: float32 [4096, 1024], P('shard')
- small_new: float32 [17408], replicated
- attention_copy: bfloat16 [1024, 8, 1024], P('shard')
- expand_copy: bfloat16 [1024, 4096], P('shard')
- shrink_copy: bfloat16 [4096, 1024], P('shard')
- attention_rows_new: float32 [8, 1024], P(None, 'shard')
- attention_cols_new: float32 [8, 1024], replicated
- expand_rows_new: float32 [1024], P('shard')
- expand_cols_new: float32 [4096], replicated
- shrink_rows_new: float32 [4096], P('shard')
- shrink_cols_new: float32 [1024], replicated
- small_moment_new: float32 [17408], replicated
- norm_stats: float32 [6], replicated
Inputs may be any that keep to these rules, and one draw needn't show every extreme that they name: Sequence s has lengths[s] valid tokens at the start of its slot; at least one sequence has exactly 1024. `encoder_lengths`: valid encoder states lie at the start of a sequence's block; at least one sequence has exactly 128. `dealt_order`: A permutation of the sequence numbers.
All inputs are finite; a program needn't handle non-finite values.
Results may differ from a plain program's by a relative error of at most 0.02.
The roundings to bfloat16 on the way count: a program that leaves them out, or rounds other values in their place, can miss the bound.
Values may be sent and summed in bfloat16 or wider, within the bound.
A program may use at most 512 MiB of HBM per device.

v0:
```python
import math

import jax
import jax.numpy as jnp
from jax import lax
from jax.experimental import pallas as pl
from jax.experimental.pallas import tpu as pltpu
from jax.sharding import PartitionSpec as P

D = 1024
HEADS = 16
HEAD_DIM = 64
FF = 4096


DECAY_RATE = 0.5
CLIP_LEVEL = 0.25
STEP_RATE = 0.1
SMALL_RATE = 0.4
OUT_GAIN = 8.0
NORM_EPS = 1e-05
FACTOR_EPS = 1e-30
MASKED = -1e30
MESH = pl.DeviceIdType.MESH
CHUNKS = 16
GATHERED = 16
EXPAND_AT = (8, 9, 11, 13)
SHRINK_AT = (10, 12, 14, 15)
MIB = 1 << 20


def layer_norm(r, norm_gain, norm_shift):
    centred = r - jnp.mean(r, axis=-1, keepdims=True)
    spread = jnp.mean(centred * centred, axis=-1, keepdims=True)
    return centred * lax.rsqrt(spread + NORM_EPS) * norm_gain + norm_shift


def gelu_exact(values):
    return jax.nn.gelu(values, approximate=False)


def unpack(small):
    extents = [D] * 6 + [FF] + [D] * 7
    pieces = []
    offset = 0
    for extent in extents:
        pieces.append(small[offset : offset + extent])
        offset = offset + extent
    return pieces


def forward_product(source, matrix):
    return jnp.dot(source, matrix, preferred_element_type=jnp.float32)


def input_product(grad_low, matrix):
    return jnp.einsum("to,io->ti", grad_low, matrix, preferred_element_type=jnp.float32)


def weight_product(source, grad_low):
    return jnp.einsum("ti,to->io", source, grad_low, preferred_element_type=jnp.float32)


def row_sum(grad_low):
    return jnp.sum(grad_low.astype(jnp.float32), axis=0)


def transposed(block):
    return block.astype(jnp.float32).T.astype(jnp.bfloat16)


def half_lanes(shape, dim):
    return lax.broadcasted_iota(jnp.int32, shape, dim)


def masked_keys(keys, length, head):
    place = half_lanes(keys.shape, 0)
    lane = half_lanes(keys.shape, 1)
    blocked = jnp.where((lane == 64 - 64 * head) & (place >= length), MASKED, 0.0)
    own = (lane >= 64 * head) & (lane < 64 * head + 64)
    return jnp.where(own, keys.astype(jnp.float32), blocked).astype(jnp.bfloat16)


def own_head(rows_t, head, fill):
    place = half_lanes(rows_t.shape, 0)
    own = (place >= 64 * head) & (place < 64 * head + 64)
    other = jnp.where(place == 64 - 64 * head, fill, 0.0)
    return jnp.where(own, rows_t.astype(jnp.float32), other).astype(jnp.bfloat16)


def product(first, second):
    return jnp.dot(first, second, preferred_element_type=jnp.float32)


def causal_mask(scores, step):
    kept = scores.shape[0] - step
    last = scores[kept:]
    allowed = half_lanes(last.shape, 0) <= half_lanes(last.shape, 1)
    last = jnp.where(allowed, last, MASKED)
    return last if kept == 0 else jnp.concatenate([scores[:kept], last], axis=0)


def attend_pair(
    causal, step, length, q_ref, k_ref, v_ref, o_ref, lse_ref, o_t, first_row=0
):
    count = q_ref.shape[0]
    q_t = transposed(q_ref[...])
    v_t = transposed(v_ref[...])
    keys = [masked_keys(k_ref[...], length, head) for head in range(2)]
    queries = [own_head(q_t, head, 1.0) for head in range(2)]
    units = [(head, start) for start in range(0, count, step) for head in range(2)]

    def scores_of(head, start):
        end = first_row + start + step if causal else k_ref.shape[0]
        return product(keys[head][:end], queries[head][:, start : start + step])

    ahead = scores_of(*units[0])
    for index, (head, start) in enumerate(units):
        scores = ahead
        if index + 1 < len(units):
            ahead = scores_of(*units[index + 1])
        rows = slice(64 * head, 64 * head + 64)
        columns = slice(start, start + step)
        if causal:
            scores = causal_mask(scores, step)
        top = jnp.max(scores, axis=0, keepdims=True)
        raised = jnp.exp(scores - top)
        total = jnp.sum(raised, axis=0, keepdims=True)
        probs = (raised * (1.0 / total)).astype(jnp.bfloat16)
        o_t[rows, columns] = product(v_t[rows, : scores.shape[0]], probs)
        place = slice(first_row + start, first_row + start + step)
        lse_ref[0, head : head + 1, place] = top + jnp.log(total)
    o_ref[...] = o_t[:, :count].T.astype(jnp.bfloat16)


def attend_back_pair(
    causal,
    step,
    length,
    q_ref,
    k_ref,
    v_ref,
    do_ref,
    lse_ref,
    dq_ref,
    dk_ref,
    dv_ref,
    put_sums,
    dq_t,
    dk_sum,
    dv_sum,
):
    key_rows = k_ref.shape[0]
    q_t = transposed(q_ref[...])
    k_t = transposed(k_ref[...])
    do_t = transposed(do_ref[...])
    values = v_ref[...]
    keys = [masked_keys(k_ref[...], length, head) for head in range(2)]
    queries = [own_head(q_t, head, 1.0) for head in range(2)]
    grads = [own_head(do_t, head, 0.0) for head in range(2)]
    count = q_ref.shape[0] // step
    units = [(head, b) for b in reversed(range(count)) for head in range(2)]

    def products_of(head, b):
        columns = slice(b * step, b * step + step)
        end = b * step + step if causal else key_rows
        scores = product(keys[head][:end], queries[head][:, columns])
        return scores, product(values[:end], grads[head][:, columns])

    ahead = products_of(*units[0])
    for index, (head, b) in enumerate(units):
        scores, d_probs = ahead
        if index + 1 < len(units):
            ahead = products_of(*units[index + 1])
        rows = slice(64 * head, 64 * head + 64)
        columns = slice(b * step, b * step + step)
        end = scores.shape[0]
        if causal:
            scores = causal_mask(scores, step)
        probs = jnp.exp(scores - lse_ref[0, head : head + 1, columns])
        weighted = probs * d_probs
        delta = jnp.sum(weighted, axis=0, keepdims=True)
        d_scores = (weighted - probs * delta).astype(jnp.bfloat16)
        dv = product(probs.astype(jnp.bfloat16), do_ref[columns, :])
        dk = product(d_scores, q_ref[columns, :])
        if b == count - 1:
            dv_sum[head, :end] = dv
            dk_sum[head, :end] = dk
        else:
            dv_sum[head, :end] += dv
            dk_sum[head, :end] += dk
        dq_t[rows, columns] = product(k_t[rows, :end], d_scores)
    first = half_lanes((key_rows, 128), 1) < 64
    dk_ref[...] = jnp.where(first, dk_sum[0, :key_rows], dk_sum[1, :key_rows]).astype(jnp.bfloat16)
    dv = jnp.where(first, dv_sum[0, :key_rows], dv_sum[1, :key_rows]).astype(jnp.bfloat16)
    dv_ref[...] = dv
    dq = (dq_t[...] * 0.125).T.astype(jnp.bfloat16)
    dq_ref[...] = dq
    put_sums(
        jnp.sum(dq.astype(jnp.float32), axis=0, keepdims=True),
        jnp.sum(dv.astype(jnp.float32), axis=0, keepdims=True),
    )


SCALARS = pl.BlockSpec(memory_space=pltpu.SMEM)


def neighbours():
    rep = lax.axis_index("rep")
    z = lax.axis_index("shard")
    core = rep % 2
    x = (rep // 2) % 2
    y = rep // 4
    other_core = (rep + 1 - 2 * core, z)
    other_x = (rep + 2 - 4 * x, z)
    other_y = (rep + 4 - 8 * y, z)
    others_z = [(rep, (z + d) % 4) for d in (1, 2, 3)]
    return core, x, y, z, other_core, other_x, other_y, others_z


def greet(devices):
    barrier = pltpu.get_barrier_semaphore()
    for device in devices:
        pl.semaphore_signal(barrier, inc=1, device_id=device, device_id_type=MESH)
    pl.semaphore_wait(barrier, len(devices))


def remote(src, dst, send, recv, device):
    return pltpu.make_async_remote_copy(
        src_ref=src, dst_ref=dst, send_sem=send, recv_sem=recv, device_id=device, device_id_type=MESH
    )


def gather_copies(refs, c, parity, places):
    piece, full, place_sem, z_send, z_recv, send, recv = refs
    core, x, y, z, other_core, other_x, other_y, others_z = places
    a = x + parity * (y - x)
    b = y + parity * (x - y)
    first = (other_x[0] + parity * (other_y[0] - other_x[0]), z)
    second = (other_y[0] + parity * (other_x[0] - other_y[0]), z)
    own = pl.ds(pl.multiple_of(core * 128 + a * 64 + b * 32, 32), 32)
    steps = (
        (own, second),
        (pl.ds(pl.multiple_of(core * 128 + a * 64, 64), 64), first),
        (pl.ds(pl.multiple_of(core * 128, 128), 128), other_core),
    )

    def local():
        return pltpu.make_async_copy(piece.at[c], full.at[c, z, own, :], place_sem.at[c])

    def line(d):
        return remote(
            piece.at[c], full.at[c, z, own, :], z_send.at[c, d], z_recv.at[c, d], others_z[d]
        )

    def pair(k):
        block = full.at[c, :, steps[k][0], :]
        return remote(block, block, send.at[k, c], recv.at[k, c], steps[k][1])

    return local, line, pair


def gather_stage(k, refs, c, parity, places):
    local, line, pair = gather_copies(refs, c, parity, places)
    if k == 0:
        local().start()
        for d in range(3):
            line(d).start()
    if k == 1:
        local().wait()
        for d in range(3):
            line(d).wait_recv()
        pair(0).start()
    if k == 2 or k == 3:
        pair(k - 2).wait_recv()
        pair(k - 1).start()
    if k == 4:
        pair(2).wait()
        pair(1).wait_send()
        pair(0).wait_send()
        for d in range(3):
            line(d).wait_send()


def gather_sems(count):
    dma = pltpu.SemaphoreType.DMA
    return [dma((count,)), dma((count, 3)), dma((count, 3)), dma((3, count)), dma((3, count))]


def hidden_blocks(values):
    split = values.reshape(values.shape[:-1] + (4, 4, 256))
    split = jnp.swapaxes(split, -3, -2)
    return split.reshape(values.shape[:-1] + (4, 1024))


def hidden_flat(blocks):
    split = blocks.reshape(blocks.shape[:-2] + (4, 4, 256))
    split = jnp.swapaxes(split, -3, -2)
    return split.reshape(blocks.shape[:-2] + (FF,))


def fold(tile):
    return jnp.sum(tile.reshape(-1, 8, tile.shape[-1]), axis=0)


GATHER_PLAN = (("z", 7.5), ("second", 7.5), ("first", 13.0), ("core", 4.0), (None, 0.0))


class GatherPlanner:
    def __init__(self, count):
        self.now = 0.0
        self.links = {"core": 0.0, "x": 0.0, "y": 0.0, "z": 0.0}
        self.stage = {c: 0 for c in range(count)}
        self.ready = {c: 0.0 for c in range(count)}
        self.opened = count

    def can(self, c):
        if self.stage[c] == 0 and c >= 3 and self.stage[c - 3] < 2:
            return False
        return self.stage[c] < 5

    def spend(self, now, **busy):
        self.now = max(self.now, now)
        for link, span in busy.items():
            self.links[link] = max(self.links[link], self.now) + span

    def emit(self, c):
        stage = self.stage[c]
        link, span = GATHER_PLAN[stage]
        first, second = ("x", "y") if c % 2 == 0 else ("y", "x")
        link = {"first": first, "second": second}.get(link, link)
        self.now = max(self.now, self.ready[c]) + 0.1
        if link is not None:
            begin = max(self.now, self.links[link])
            self.links[link] = begin + span - 1.0
            self.ready[c] = begin + span
        self.stage[c] = stage + 1
        return (stage, c)

    def tick(self, spent):
        self.now += spent
        events = []
        progress = True
        while progress:
            progress = False
            for c in range(self.opened):
                if self.can(c) and self.ready[c] <= self.now:
                    events.append(self.emit(c))
                    progress = True
        return events

    def until(self, c):
        events = []
        while self.stage[c] < 5:
            choices = [i for i in range(self.opened) if self.can(i)]
            best = min(choices, key=lambda i: (self.ready[i], i))
            events.append(self.emit(best))
        return events


ERFC_SERIES = (
    0.08459648489952087,
    0.085321806371212,
    0.0743890032172203,
    0.10671534389257431,
    -0.04577348381280899,
    0.27184805274009705,
    -0.2545455992221832,
    0.24207571148872375,
    -0.06462734192609787,
)


def gelu_parts(u):
    bell = jnp.exp(-0.5 * u * u)
    t = 1.0 / (1.0 + (0.3 * math.sqrt(0.5)) * jnp.abs(u))
    series = ERFC_SERIES[8]
    for coefficient in ERFC_SERIES[7::-1]:
        series = series * t + coefficient
    tail = series * t * bell
    share = jnp.where(u < 0.0, tail, 1.0 - tail)
    return u * share, share + u * (bell * (1.0 / math.sqrt(2.0 * math.pi)))


def norm_parts(values):
    centred = values - jnp.mean(values, axis=1, keepdims=True)
    spread = jnp.mean(centred * centred, axis=1, keepdims=True)
    scale = lax.rsqrt(spread + NORM_EPS)
    return centred * scale, scale


def forward_kernel(
    order_ref,
    lengths_ref,
    state_lengths_ref,
    tokens_ref,
    att_ref,
    exp_ref,
    shr_ref,
    e_ref,
    cot_ref,
    par,
    x_out,
    full_ref,
    q_out,
    k_out,
    v_out,
    o_out,
    lse_out,
    cq_out,
    ck_out,
    cv_out,
    oc_out,
    lse_cross_out,
    r1_out,
    r2_out,
    h1_out,
    h2_out,
    g_out,
    gp_out,
    y_out,
    dm_out,
    d_third_out,
    small_out,
    pool,
    acc,
    held,
    o_t,
    lse_held,
    states,
    x_held,
    spread,
    picked,
    piece_ref,
    att_in,
    exp_in,
    shr_in,
    prepare_sem,
    load_sem,
    store_sem,
    state_sem,
    acc_sem,
    spread_send,
    spread_recv,
    back_send,
    back_recv,
    *gather_sem,
):
    places = neighbours()
    refs = (piece_ref, full_ref) + gather_sem
    planner = GatherPlanner(GATHERED)
    me = lax.axis_index("rep") * 4 + places[3]
    length = lengths_ref[me]

    core, x, y = places[0:3]

    def own_row(parity):
        a = x + parity * (y - x)
        b = y + parity * (x - y)
        return core * 128 + a * 64 + b * 32

    prepare = []
    for p in range(2):
        for lane in range(8):
            rows = pl.ds(pl.multiple_of(own_row(p) * 8, 256), 256)
            prepare.append((att_ref.at[rows, pl.ds(lane * 128, 128)], att_in.at[p, lane]))
        rows = pl.ds(pl.multiple_of(own_row(p), 32), 32)
        prepare.append((exp_ref.at[rows, :], exp_in.at[p]))
    for j in range(4):
        rows = pl.ds(pl.multiple_of(j * 256 + own_row(SHRINK_AT[j] % 2), 32), 32)
        prepare.append((shr_ref.at[rows, :], shr_in.at[j]))
    prepare = [
        pltpu.make_async_copy(source, target, prepare_sem.at[i])
        for i, (source, target) in enumerate(prepare)
    ]

    def make_pieces():
        for copy in prepare:
            copy.wait()
        for c in range(8):
            for lane in range(8):
                tile = att_in[c % 2, lane, pl.ds(c, 32, stride=8), :]
                piece_ref[c, :, lane * 128 : lane * 128 + 128] = tile.astype(jnp.bfloat16)
        for j in range(4):
            c = EXPAND_AT[j]
            for s in range(4):
                start = s * 1024 + j * 256
                tile = exp_in[c % 2, :, start : start + 256]
                piece_ref[c, :, s * 256 : s * 256 + 256] = tile.astype(jnp.bfloat16)
            piece_ref[SHRINK_AT[j]] = shr_in[j].astype(jnp.bfloat16)

    def device(offset):
        j = lax.rem(me + offset, 32)
        return j, (j // 4, j % 4)

    def spread_copy(offset):
        j, target = device(offset)
        return remote(
            tokens_ref.at[j],
            spread.at[me],
            spread_send.at[offset],
            spread_recv.at[offset],
            target,
        )

    def back_copy(offset):
        return remote(
            picked.at[offset],
            x_held.at[me],
            back_send.at[offset],
            back_recv.at[offset],
            device(offset)[1],
        )

    def own_spread():
        return pltpu.make_async_copy(tokens_ref.at[me], spread.at[me], spread_recv.at[0])

    def own_back():
        return pltpu.make_async_copy(picked.at[0], x_held.at[me], back_recv.at[0])

    def each_other(act):
        def body(offset, carry):
            act(offset)
            return carry

        lax.fori_loop(1, 32, body, 0)

    def turn_back():
        own_spread().wait()
        each_other(lambda offset: spread_copy(offset).wait())
        picked[0] = spread[order_ref[me]]
        own_back().start()

        def pick(offset):
            picked[offset] = spread[order_ref[device(offset)[0]]]
            back_copy(offset).start()

        each_other(pick)

    def emit_all(events):
        for stage, c in events:
            gather_stage(stage, refs, c, c % 2, places)

    def tick(spent):
        emit_all(planner.tick(spent))

    def load(slot, source):
        return pltpu.make_async_copy(source, pool.at[slot], load_sem.at[slot])

    def store(slot, target):
        return pltpu.make_async_copy(pool.at[slot], target, store_sem.at[slot])

    def product_into(left, right, put):
        def body(i, carry):
            n = pl.multiple_of(i * 256, 256)
            put(n, product(left(), pool[right, :, pl.ds(n, 256)]))
            return carry

        lax.fori_loop(0, 4, body, 0)

    def row(index, n):
        return par[index : index + 1, pl.ds(n, 256)]

    def put_low(slot, offset=None, scale=None):
        def put(n, value):
            if offset is not None:
                value = value + row(offset, n)
            if scale is not None:
                value = value * scale
            pool[slot, :, pl.ds(n, 256)] = value.astype(jnp.bfloat16)

        return put

    def put_acc(offset):
        def put(n, value):
            acc[:, pl.ds(n, 256)] = value + row(offset, n)

        return put

    def load_weight(c, slot):
        target = pool.at[slot].reshape(4, 256, D)
        return pltpu.make_async_copy(full_ref.at[c], target, load_sem.at[slot])

    def weight(c, slot):
        emit_all(planner.until(c))
        return load_weight(c, slot)

    def attend_loop(causal, step, valid, query, key, value, out, spent, rows, key_rows):
        ahead = [planner.tick(spent) for _ in range(8)]
        first_row, count = rows

        def body(i, carry):
            lanes = pl.ds(pl.multiple_of(i * 128, 128), 128)
            attend_pair(
                causal,
                step,
                valid,
                query.at[pl.ds(first_row, count), lanes],
                key.at[pl.ds(0, key_rows), lanes],
                value.at[pl.ds(0, key_rows), lanes],
                out.at[pl.ds(first_row, count), lanes],
                lse_held.at[pl.ds(i, 1)],
                o_t,
                first_row,
            )
            for n in range(8):
                if ahead[n]:

                    @pl.when(i == n)
                    def _(events=ahead[n]):
                        emit_all(events)

            return carry

        lax.fori_loop(0, 8, body, 0)

    TILE = 128

    def over_rows(sums, body):
        zero = jnp.zeros((8, D), jnp.float32)

        def step(i, carry):
            r = pl.multiple_of(i * TILE, TILE)
            place = half_lanes((TILE, 1), 0) + r
            usable = (place < length).astype(jnp.float32)
            terms = body(pl.ds(r, TILE), usable)
            return tuple(c + fold(t) for c, t in zip(carry, terms))

        totals = lax.fori_loop(0, D // TILE, step, (zero,) * sums)
        return [jnp.sum(t, axis=0, keepdims=True) for t in totals]

    lane = half_lanes((1, D), 1)

    def square_at(index, total):
        small_out[17:18, :] += jnp.where(lane == index, jnp.sum(total), 0.0)

    for copy in prepare:
        copy.start()
    barrier = pltpu.get_barrier_semaphore()

    def greet_one(offset):
        pl.semaphore_signal(barrier, inc=1, device_id=device(offset)[1], device_id_type=MESH)

    each_other(greet_one)
    pl.semaphore_wait(barrier, 31)
    own_spread().start()
    each_other(lambda offset: spread_copy(offset).start())
    make_pieces()
    planner.opened = 3
    tick(0.5)
    planner.spend(3.0, z=42.0, x=21.0, y=21.0)
    e_load = pltpu.make_async_copy(e_ref, states.at[2], state_sem.at[2])
    e_load.start()
    load(9, cot_ref).start()
    small_out[...] = jnp.zeros_like(small_out)
    turn_back()
    planner.spend(56.0, z=42.0, x=21.0, y=21.0)
    planner.opened = 5
    for i in range(3):
        weight(i, 1 + i).start()
    own_back().wait()
    each_other(lambda offset: back_copy(offset).wait())
    planner.spend(112.0)
    planner.opened = GATHERED
    tick(0.5)
    x_store = pltpu.make_async_copy(x_held, x_out, acc_sem.at[1])
    x_store.start()

    for i, (slot, offset, scale) in enumerate(((4, 0, 0.125), (5, None, None), (6, 1, None))):
        load_weight(i, 1 + i).wait()
        product_into(lambda: x_held[...].reshape(1024, D), 1 + i, put_low(slot, offset, scale))
        store(slot, (q_out, k_out, v_out)[i]).start()
        tick(2.5)
    refs_held = [pool.at[slot] for slot in (4, 5, 6, 7)]
    attend_loop(True, 256, length, *refs_held, 4.5, (0, 1024), 1024)
    store(7, o_out).start()
    lse_copy = pltpu.make_async_copy(lse_held, lse_out, state_sem.at[3])
    lse_copy.start()
    w_copy = weight(3, 1)
    w_copy.start()
    w_copy.wait()
    product_into(lambda: pool[7], 1, put_acc(2))
    tick(2.5)
    store(4, q_out).wait()

    def first_norm(rows, usable):
        held_rows = pl.ds(pl.multiple_of(rows.start // 32, TILE // 32), TILE // 32)
        x = x_held[held_rows].reshape(TILE, D).astype(jnp.float32)
        a = acc[rows, :]
        total = x + a
        acc[rows, :] = total
        h = norm_parts(total)[0] * par[11:12, :] + par[12:13, :]
        held[rows, :] = h
        pool[4, rows, :] = h.astype(jnp.bfloat16)
        return usable * x * x, usable * a * a, usable * h * h

    for index, total in enumerate(over_rows(3, first_norm)):
        square_at(index, total)
    store(4, h1_out).start()
    r1_copy = pltpu.make_async_copy(acc, r1_out, acc_sem.at[0])
    r1_copy.start()
    tick(4.0)

    for c, slot in ((4, 2), (5, 3), (6, 1)):
        weight(c, slot).start()
    store(5, k_out).wait()
    load_weight(4, 2).wait()
    product_into(lambda: pool[4], 2, put_low(5, 3, 0.125))
    store(5, cq_out).start()
    w_copy = weight(7, 2)
    w_copy.start()
    tick(2.5)
    e_load.wait()
    load_weight(5, 3).wait()
    load_weight(6, 1).wait()

    def put_keys(n, value):
        states[0, :, pl.ds(n, 256)] = value.astype(jnp.bfloat16)

    def put_values(n, value):
        states[1, :, pl.ds(n, 256)] = (value + row(4, n)).astype(jnp.bfloat16)

    product_into(lambda: states[2], 3, put_keys)
    product_into(lambda: states[2], 1, put_values)
    state_stores = [
        pltpu.make_async_copy(states.at[0], ck_out, state_sem.at[0]),
        pltpu.make_async_copy(states.at[1], cv_out, state_sem.at[1]),
    ]
    for copy in state_stores:
        copy.start()
    tick(1.0)
    store(6, v_out).wait()
    lse_copy.wait()
    attend_loop(
        False,
        512,
        state_lengths_ref[me],
        pool.at[5],
        states.at[0],
        states.at[1],
        pool.at[6],
        1.6,
        (0, 1024),
        128,
    )
    store(6, oc_out).start()
    lse_copy = pltpu.make_async_copy(lse_held, lse_cross_out, state_sem.at[3])
    lse_copy.start()
    w_copy.wait()
    r1_copy.wait()
    product_into(lambda: pool[6], 2, put_acc(5))
    tick(2.5)
    weight(EXPAND_AT[0], 0).start()
    store(7, o_out).wait()

    def second_norm(rows, usable):
        c = acc[rows, :]
        total = held[rows, :] + c
        acc[rows, :] = total
        h = norm_parts(total)[0] * par[13:14, :] + par[14:15, :]
        held[rows, :] = h
        pool[7, rows, :] = h.astype(jnp.bfloat16)
        return usable * c * c, usable * h * h

    for index, total in enumerate(over_rows(2, second_norm)):
        square_at(3 + index, total)
    store(7, h2_out).start()
    r2_copy = pltpu.make_async_copy(acc, r2_out, acc_sem.at[0])
    r2_copy.start()
    tick(4.0)

    store(4, h1_out).wait()
    store(5, cq_out).wait()
    g_slots, slope_slots = (4, 6), (5, 8)
    r2_copy.wait()
    store(6, oc_out).wait()
    for j in range(5):
        if j > 1:
            store(g_slots[j % 2], g_out.at[j - 2]).wait()
            store(slope_slots[j % 2], gp_out.at[j - 2]).wait()
        if j < 4:
            load_weight(EXPAND_AT[j], j % 2).wait()
        if j > 0:
            load_weight(SHRINK_AT[j - 1], 2 + (j - 1) % 2).wait()

        def body(i, carry, j=j):
            n = pl.multiple_of(i * 256, 256)
            here = pl.ds(n, 256)
            if j < 4:
                offset = par[pl.ds(6 + i, 1), j * 256 : j * 256 + 256]
                u = product(pool[7], pool[j % 2, :, here]) + offset
            if j > 0:
                more = product(pool[g_slots[(j - 1) % 2]], pool[2 + (j - 1) % 2, :, here])
                if j == 1:
                    acc[:, here] = more + row(10, n)
                else:
                    acc[:, here] += more
            if j < 4:
                g, slope = gelu_parts(u)
                pool[g_slots[j % 2], :, here] = g.astype(jnp.bfloat16)
                pool[slope_slots[j % 2], :, here] = slope.astype(jnp.bfloat16)
            return carry

        ahead = [planner.tick(2.2 if j < 4 else 0.6) for _ in range(4)]

        def body_and_stages(i, carry, body=body, ahead=ahead):
            body(i, carry)
            for n in range(4):
                if ahead[n]:

                    @pl.when(i == n)
                    def _(events=ahead[n]):
                        emit_all(events)

            return carry

        lax.fori_loop(0, 4, body_and_stages, 0)
        if j < 4:
            store(g_slots[j % 2], g_out.at[j]).start()
            store(slope_slots[j % 2], gp_out.at[j]).start()
        if j < 3:
            weight(EXPAND_AT[j + 1], (j + 1) % 2).start()
        if j < 4:
            weight(SHRINK_AT[j], 2 + j % 2).start()

    load(9, cot_ref).wait()

    def third_norm(rows, usable):
        m = acc[rows, :]
        unit, scale = norm_parts(held[rows, :] + m)
        gain = par[15:16, :]
        pool[0, rows, :] = (unit * gain + par[16:17, :]).astype(jnp.bfloat16)
        grad = pool[9, rows, :].astype(jnp.float32) * usable
        inner = grad * gain
        first = jnp.mean(inner, axis=1, keepdims=True)
        second = jnp.mean(inner * unit, axis=1, keepdims=True)
        back = scale * (inner - first - unit * second)
        acc[rows, :] = back
        low = back.astype(jnp.bfloat16)
        pool[1, rows, :] = low
        return usable * m * m, grad * unit, grad, low.astype(jnp.float32)

    m_total, gain_sum, shift_sum, offset_sum = over_rows(4, third_norm)
    square_at(5, m_total)
    small_out[15:16, :] = gain_sum
    small_out[16:17, :] = shift_sum
    small_out[10:11, :] = offset_sum
    last = [
        store(0, y_out),
        store(1, dm_out),
        pltpu.make_async_copy(acc, d_third_out, acc_sem.at[0]),
    ]
    for copy in last:
        copy.start()
    for c in range(GATHERED):
        emit_all(planner.until(c))
    for copy in last + state_stores + [lse_copy, x_store]:
        copy.wait()
    store(7, h2_out).wait()
    store(6, g_out.at[3]).wait()
    store(8, gp_out.at[3]).wait()


def forward(scalars, tokens, weights, states, cotangent, params):
    any_space = pl.BlockSpec(memory_space=pl.ANY)
    vmem = pl.BlockSpec(memory_space=pltpu.VMEM)
    shape = jax.ShapeDtypeStruct
    dma = pltpu.SemaphoreType.DMA
    low = jnp.bfloat16
    wide = jnp.float32
    square = shape((1024, D), low)
    square_wide = shape((1024, D), wide)
    lse = shape((8, 8, 1024), wide)
    short = shape((128, D), low)
    blocks = shape((4, 1024, D), low)
    outs = (
        shape((32, 32, D), low),
        shape((GATHERED, 4, 256, D), low),
        square,
        square,
        square,
        square,
        lse,
        square,
        short,
        short,
        square,
        lse,
        square_wide,
        square_wide,
        square,
        square,
        blocks,
        blocks,
        square,
        square,
        square_wide,
        shape((24, D), wide),
    )
    return pl.pallas_call(
        forward_kernel,
        out_shape=outs,
        in_specs=[SCALARS] * 3 + [any_space] * 6 + [vmem],
        out_specs=(any_space,) * 21 + (vmem,),
        scratch_shapes=[
            pltpu.VMEM((10, 1024, D), low),
            pltpu.VMEM((1024, D), wide),
            pltpu.VMEM((1024, D), wide),
            pltpu.VMEM((128, 1024), wide),
            pltpu.VMEM((8, 8, 1024), wide),
            pltpu.VMEM((3, 128, D), low),
            pltpu.VMEM((32, 32, D), low),
            pltpu.VMEM((32, 32, D), low),
            pltpu.VMEM((32, 32, D), low),
            pltpu.VMEM((GATHERED, 32, D), low),
            pltpu.VMEM((2, 8, 256, 128), wide),
            pltpu.VMEM((2, 32, FF), wide),
            pltpu.VMEM((4, 32, D), wide),
            dma((22,)),
            dma((10,)),
            dma((10,)),
            dma((4,)),
            dma((2,)),
            dma((32,)),
            dma((32,)),
            dma((32,)),
            dma((32,)),
        ]
        + gather_sems(GATHERED),
        compiler_params=pltpu.CompilerParams(
            collective_id=3, has_side_effects=True, vmem_limit_bytes=62 * MIB
        ),
    )(*scalars, tokens.reshape(32, 32, D), *weights, states, cotangent, params)


def add_blocks(target, first, second, planes, rows, step):
    per_plane = rows // step

    def body(i, carry):
        s = i // per_plane
        r = pl.multiple_of((i % per_plane) * step, step)
        target(s, r, first(s, r) + second(s, r))
        return carry

    lax.fori_loop(0, planes * per_plane, body, 0)


POOL = 8
G_SLOTS = 3
R_SLOTS = 4
PLAN = {"core": 3.5, "load": 1.8, "a": 13.5, "b": 7.5, "z": 7.5, "bb": 3.0, "ba": 5.0, "bc": 2.5}


class Planner:
    def __init__(self):
        self.now = 0.0
        self.links = {"core": 0.0, "x": 0.0, "y": 0.0, "z": 0.0, "load": 0.0}
        self.stage = {}
        self.ready = {}

    def link_of(self, c, stage):
        first, second = ("x", "y") if c % 2 == 0 else ("y", "x")
        return {
            0: ("core", "core"),
            1: ("load", "load"),
            2: (first, "a"),
            3: (second, "b"),
            4: ("z", "z"),
            5: (second, "bb"),
            6: (first, "ba"),
            7: ("core", "bc"),
            8: (None, None),
        }[stage]

    def can(self, c):
        stage = self.stage[c]
        if stage > 8:
            return False
        if stage == 1 and c >= R_SLOTS and self.stage[c - R_SLOTS] <= 3:
            return False
        return True

    def emit(self, c):
        stage = self.stage[c]
        link, kind = self.link_of(c, stage)
        self.now = max(self.now, self.ready[c]) + {2: 0.8, 3: 0.5, 4: 0.3, 5: 0.2}.get(stage, 0.1)
        if link is not None:
            begin = max(self.now, self.links[link])
            span = PLAN[kind]
            self.links[link] = begin + span - 1.0
            self.ready[c] = begin + span
        self.stage[c] = stage + 1
        return (stage, c)

    def tick(self, spent):
        self.now += spent
        events = []
        progress = True
        while progress:
            progress = False
            for c in sorted(self.stage):
                if self.can(c) and self.ready[c] <= self.now:
                    events.append(self.emit(c))
                    progress = True
        return events

    def produce(self, c):
        self.stage[c] = 0
        self.ready[c] = self.now
        return [self.emit(c)]

    def until(self, done):
        events = []
        while not done():
            choices = [c for c in sorted(self.stage) if self.can(c)]
            c = min(choices, key=lambda i: (self.ready[i], i))
            events.append(self.emit(c))
        return events

    def free_slot(self, c):
        before = c - G_SLOTS
        if before < 0:
            return []
        return self.until(lambda: self.stage[before] > 2)

    def drain(self, tasks, spent):
        events = []
        waiting = list(tasks)
        while waiting or any(s <= 8 for s in self.stage.values()):
            choices = [c for c in sorted(self.stage) if self.can(c)]
            best = min(choices, key=lambda i: (self.ready[i], i)) if choices else None
            open_tasks = [t for t in waiting if all(self.stage[c] > 8 for c in t[0])]
            if open_tasks and (best is None or self.ready[best] > self.now):
                task = open_tasks[0]
                waiting.remove(task)
                self.now += spent
                events.append(("task", task[1]))
            else:
                events.append(self.emit(best))
        return events


def backward_kernel(
    lengths_ref,
    state_lengths_ref,
    dm_ref,
    d_third_ref,
    g_ref,
    gp_ref,
    full_ref,
    h2_ref,
    h1_ref,
    x_in_ref,
    e_ref,
    oc_ref,
    o_ref,
    r1_ref,
    r2_ref,
    q_ref,
    k_ref,
    v_ref,
    cq_ref,
    ck_ref,
    cv_ref,
    lse_ref,
    lse_cross_ref,
    gains_ref,
    small_ref,
    rows_ref,
    cols_ref,
    token_grad_ref,
    state_grad_ref,
    out_ref,
    totals_ref,
    rows_out,
    cols_out,
    scale_out,
    half,
    pool,
    acc,
    made,
    summed,
    quarter,
    eighth,
    pieces,
    stream,
    dq_t,
    dk_sum,
    dv_sum,
    lse_held,
    states,
    states_t,
    small,
    small_in,
    small_sum,
    small_z,
    part,
    whole,
    load_sem,
    stream_sem,
    state_sem,
    half_sem,
    scan_sem,
    line_send_sem,
    line_recv_sem,
    send_sem,
    recv_sem,
    z_send_sem,
    z_recv_sem,
    place_sem,
    small_send_sem,
    small_recv_sem,
):
    core, x, y, z, other_core, other_x, other_y, others_z = neighbours()
    me = lax.axis_index("rep") * 4 + z
    kept = pl.multiple_of(core * 128, 128)
    given = pl.multiple_of(128 - core * 128, 128)
    planner = Planner()
    place_of = (12, 8, 13, 9, 14, 10, 15, 11, 7, 4, 5, 6, 3, 0, 1, 2)

    def axes(c):
        if c % 2 == 0:
            return x, y, other_x, other_y
        return y, x, other_y, other_x

    def core_copy(c):
        source = made.at[c % G_SLOTS, :, pl.ds(given, 128), :]
        return remote(source, half.at[c], send_sem.at[0, c], recv_sem.at[0, c], other_core)

    def half_copy(c):
        return pltpu.make_async_copy(
            half.at[c], summed.at[c % R_SLOTS], half_sem.at[c % R_SLOTS]
        )

    def first_copy(c):
        a, b, first, second = axes(c)
        rows = pl.ds(pl.multiple_of(64 - a * 64, 64), 64)
        source = summed.at[c % R_SLOTS, :, rows, :]
        return remote(source, quarter.at[c], send_sem.at[1, c], recv_sem.at[1, c], first)

    def second_copy(c):
        a, b, first, second = axes(c)
        rows = pl.ds(pl.multiple_of(32 - b * 32, 32), 32)
        source = quarter.at[c, :, rows, :]
        return remote(source, eighth.at[c], send_sem.at[2, c], recv_sem.at[2, c], second)

    def z_copy(c, d):
        device = others_z[d]
        return remote(
            eighth.at[c, device[1]],
            pieces.at[c, d],
            z_send_sem.at[c, d],
            z_recv_sem.at[c, d],
            device,
        )

    def own_rows_of(c):
        a, b, first, second = axes(c)
        return pl.ds(pl.multiple_of(core * 128 + a * 64 + b * 32, 32), 32)

    def place_copy(c):
        return pltpu.make_async_copy(
            pieces.at[c, 0], out_ref.at[place_of[c], own_rows_of(c), :], place_sem.at[c]
        )

    def back_second(c):
        device = axes(c)[3]
        target = out_ref.at[place_of[c], own_rows_of(c), :]
        return remote(pieces.at[c, 0], target, send_sem.at[3, c], recv_sem.at[3, c], device)

    def back_first(c):
        a, b, first, second = axes(c)
        block = out_ref.at[place_of[c], pl.ds(pl.multiple_of(core * 128 + a * 64, 64), 64), :]
        return remote(block, block, send_sem.at[4, c], recv_sem.at[4, c], first)

    def back_core(c):
        block = out_ref.at[place_of[c], pl.ds(kept, 128), :]
        return remote(block, block, send_sem.at[5, c], recv_sem.at[5, c], other_core)

    def emit(stage, c):
        a, b, first, second = axes(c)
        slot = c % R_SLOTS
        if stage == 0:
            core_copy(c).start()
        if stage == 1:
            if c >= R_SLOTS:
                first_copy(c - R_SLOTS).wait_send()
            core_copy(c).wait_recv()
            half_copy(c).start()
        if stage == 2:
            half_copy(c).wait()

            def put(s, r, value):
                summed[slot, s, pl.ds(r, 32), :] = value

            add_blocks(
                put,
                lambda s, r: summed[slot, s, pl.ds(r, 32), :],
                lambda s, r: made[c % G_SLOTS, s, pl.ds(pl.multiple_of(kept + r, 32), 32), :],
                4,
                128,
                32,
            )
            first_copy(c).start()
            core_copy(c).wait_send()
        if stage == 3:
            first_copy(c).wait_recv()

            def put(s, r, value):
                quarter[c, s, pl.ds(r, 32), :] = value

            add_blocks(
                put,
                lambda s, r: quarter[c, s, pl.ds(r, 32), :],
                lambda s, r: summed[slot, s, pl.ds(pl.multiple_of(a * 64 + r, 32), 32), :],
                4,
                64,
                32,
            )
            second_copy(c).start()
        if stage == 4:
            second_copy(c).wait_recv()

            def put(s, r, value):
                eighth[c, s, pl.ds(r, 32), :] = value

            add_blocks(
                put,
                lambda s, r: eighth[c, s, pl.ds(r, 32), :],
                lambda s, r: quarter[c, s, pl.ds(pl.multiple_of(b * 32 + r, 32), 32), :],
                4,
                32,
                32,
            )
            for d in range(3):
                z_copy(c, d).start()
        if stage == 5:
            for d in range(3):
                z_copy(c, d).wait_recv()
            total = eighth[c, z].astype(jnp.float32)
            for d in range(3):
                total = total + pieces[c, d].astype(jnp.float32)
            pieces[c, 0] = total.astype(jnp.bfloat16)
            back_second(c).start()
            place_copy(c).start()
        if stage == 6:
            place_copy(c).wait()
            back_second(c).wait_recv()
            back_first(c).start()
        if stage == 7:
            back_first(c).wait_recv()
            back_core(c).start()
        if stage == 8:
            back_core(c).wait()
            back_first(c).wait_send()
            back_second(c).wait_send()
            for d in range(3):
                z_copy(c, d).wait_send()
            second_copy(c).wait_send()
            if c >= CHUNKS - R_SLOTS:
                first_copy(c).wait_send()

    def emit_all(events):
        for stage, c in events:
            emit(stage, c)

    def tick(spent):
        emit_all(planner.tick(spent))

    def produced(c, spent):
        planner.now += spent
        emit_all(planner.produce(c))
        emit_all(planner.tick(0.0))

    def load(slot, source):
        return pltpu.make_async_copy(source, pool.at[slot], load_sem.at[slot])

    def state_load(index, source):
        return pltpu.make_async_copy(source, states.at[index], state_sem.at[index])

    def turn_tile(target, source):
        def turn(n):
            pool[target, pl.ds(n, 256), :] = pool[source, :, pl.ds(n, 256)].T

        return turn

    def transpose_into(target, source):
        turn = turn_tile(target, source)

        def body(i, carry):
            turn(pl.multiple_of(i * 256, 256))
            return carry

        lax.fori_loop(0, 4, body, 0)

    def product_nn(left, right, put, beside=None):
        def body(i, carry):
            n = pl.multiple_of(i * 256, 256)
            if beside is not None:
                beside(n)
            put(n, product(left(), right(n)))
            return carry

        lax.fori_loop(0, 4, body, 0)

    def product_nt(left, right, put, beside=None):
        def body(i, carry):
            n = pl.multiple_of(i * 256, 256)
            if beside is not None:
                beside(n)
            put(
                n,
                lax.dot_general(
                    left(),
                    right(n),
                    (((1,), (1,)), ((), ())),
                    preferred_element_type=jnp.float32,
                ),
            )
            return carry

        lax.fori_loop(0, 4, body, 0)

    def columns_of(slot):
        return lambda n: pool[slot, :, pl.ds(n, 256)]

    def rows_of(slot):
        return lambda n: pool[slot, pl.ds(n, 256), :]

    def weight_grad(slot_in_made, left, right, beside=None):
        def put(n, value):
            low = value.astype(jnp.bfloat16).reshape(4, 256, 256)
            made[slot_in_made, :, :, pl.ds(n, 256)] = low

        product_nn(left, right, put, beside)

    def add_to_acc(n, value):
        acc[:, pl.ds(n, 256)] += value

    def put_in(slot):
        def put(n, value):
            pool[slot, :, pl.ds(n, 256)] = value.astype(jnp.bfloat16)

        return put

    def norm_back(source, gain_row, gain_at, shift_at, offset_at, target):
        tiles = 8
        rows = 1024 // tiles

        def fetch(i):
            place = pl.ds(pl.multiple_of(i * rows, rows), rows)
            return pltpu.make_async_copy(
                source.at[place, :], stream.at[i % 2], stream_sem.at[i % 2]
            )

        fetch(0).start()

        def body(i, carry):
            gain_sum, shift_sum, offset_sum = carry

            @pl.when(i + 1 < tiles)
            def _():
                fetch(i + 1).start()

            fetch(i).wait()
            r = pl.multiple_of(i * rows, rows)
            values = stream[i % 2]
            centred = values - jnp.mean(values, axis=1, keepdims=True)
            spread = jnp.mean(centred * centred, axis=1, keepdims=True)
            scale = lax.rsqrt(spread + NORM_EPS)
            unit = centred * scale
            grad = acc[pl.ds(r, rows), :]
            inner = grad * gains_ref[gain_row : gain_row + 1, :]
            first = jnp.mean(inner, axis=1, keepdims=True)
            second = jnp.mean(inner * unit, axis=1, keepdims=True)
            back = scale * (inner - first - unit * second)
            acc[pl.ds(r, rows), :] = back
            low = back.astype(jnp.bfloat16)
            pool[target, pl.ds(r, rows), :] = low
            return (
                gain_sum + fold(grad * unit),
                shift_sum + fold(grad),
                offset_sum + fold(low.astype(jnp.float32)),
            )

        zero = jnp.zeros((8, D), jnp.float32)
        sums = lax.fori_loop(0, tiles, body, (zero, zero, zero))
        for row, value in zip((gain_at, shift_at, offset_at), sums):
            small[row : row + 1, :] = jnp.sum(value, axis=0, keepdims=True)

    greet([other_core, other_x, other_y] + others_z)
    load(0, dm_ref).start()
    load(6, h2_ref).start()
    load(2, full_ref.at[SHRINK_AT[0]]).start()
    load(3, gp_ref.at[0]).start()
    load(4, g_ref.at[0]).start()
    load(5, full_ref.at[EXPAND_AT[0]]).start()
    acc_load = pltpu.make_async_copy(d_third_ref, acc, place_sem.at[0])
    acc_load.start()
    small[...] = small_ref[...]
    load(6, h2_ref).wait()
    transpose_into(1, 6)
    load(0, dm_ref).wait()
    acc_load.wait()

    planner.now = 4.0
    plan = []
    for j in range(4):
        entry = []
        planner.now += 3.5
        entry.append(planner.tick(0.0) + planner.free_slot(2 * j))
        planner.now += 2.5
        entry.append(planner.produce(2 * j) + planner.tick(0.0) + planner.free_slot(2 * j + 1))
        planner.now += 2.5
        entry.append(planner.produce(2 * j + 1) + planner.tick(0.0))
        entry.append(planner.tick(2.5))
        plan.append(entry)

    def emit_planned(j, place):
        for n in range(4):
            events = plan[n][place]
            if events:

                @pl.when(j == n)
                def _(events=events):
                    emit_all(events)

    def block(j, carry):
        last = j == 3
        load(2, full_ref.at[SHRINK_AT[0]]).wait()
        load(3, gp_ref.at[0]).wait()

        def put_pre(n, value):
            low = (value * pool[3, :, pl.ds(n, 256)].astype(jnp.float32)).astype(jnp.bfloat16)
            pool[7, :, pl.ds(n, 256)] = low
            small[pl.ds(6 + n // 256, 1), pl.ds(pl.multiple_of(j * 256, 256), 256)] = jnp.sum(
                low.astype(jnp.float32), axis=0, keepdims=True
            )

        load(4, g_ref.at[0]).wait()
        product_nt(lambda: pool[0], rows_of(2), put_pre, turn_tile(6, 4))

        @pl.when(jnp.logical_not(last))
        def _():
            load(2, full_ref.at[SHRINK_AT[0] + 2 * (j + 1) - (j + 1) // 3]).start()
            load(3, gp_ref.at[j + 1]).start()

        @pl.when(last)
        def _():
            load(2, full_ref.at[7]).start()
            load(3, cq_ref).start()

        emit_planned(j, 0)

        @pl.when(jnp.logical_not(last))
        def _():
            load(4, g_ref.at[j + 1]).start()

        @pl.when(last)
        def _():
            load(4, oc_ref).start()

        weight_grad((2 * j) % G_SLOTS, lambda: pool[6], columns_of(0))
        emit_planned(j, 1)
        weight_grad((2 * j + 1) % G_SLOTS, lambda: pool[1], columns_of(7))
        emit_planned(j, 2)
        load(5, full_ref.at[EXPAND_AT[0]]).wait()
        product_nt(lambda: pool[7], rows_of(5), add_to_acc)

        @pl.when(jnp.logical_not(last))
        def _():
            load(5, full_ref.at[EXPAND_AT[1] + 2 * j]).start()

        @pl.when(last)
        def _():
            load(5, full_ref.at[4]).start()

        emit_planned(j, 3)
        return carry

    lax.fori_loop(0, 4, block, 0)

    load(7, h1_ref).start()
    state_loads = [state_load(0, ck_ref), state_load(1, cv_ref), state_load(2, e_ref)]
    for copy in state_loads:
        copy.start()
    lse_load = pltpu.make_async_copy(lse_cross_ref, lse_held, state_sem.at[3])
    lse_load.start()
    norm_back(r2_ref, 13, 13, 14, 5, 0)
    tick(4.0)
    load(4, oc_ref).wait()
    load(2, full_ref.at[7]).wait()
    product_nt(lambda: pool[0], rows_of(2), put_in(4), turn_tile(6, 4))
    load(2, full_ref.at[3]).start()
    tick(2.5)
    emit_all(planner.free_slot(8))
    load(7, h1_ref).wait()
    weight_grad(8 % G_SLOTS, lambda: pool[6], columns_of(0), turn_tile(1, 7))
    load(6, o_ref).start()
    load(7, full_ref.at[5]).start()
    produced(8, 2.5)
    load(3, cq_ref).wait()
    for copy in state_loads:
        copy.wait()
    lse_load.wait()

    def attend_loop(causal, step, length, query, key, value, grad, rows, spent, span=(0, 8)):
        ahead = {n: planner.tick(spent) for n in range(*span)}

        def body(i, carry):
            lanes = pl.ds(pl.multiple_of(i * 128, 128), 128)

            def sums(dq, dv):
                small[rows[0] : rows[0] + 1, lanes] = dq
                small[rows[1] : rows[1] + 1, lanes] = dv

            attend_back_pair(
                causal,
                step,
                length,
                query.at[:, lanes],
                key.at[:, lanes],
                value.at[:, lanes],
                grad.at[:, lanes],
                lse_held.at[pl.ds(i, 1)],
                query.at[:, lanes],
                key.at[:, lanes],
                value.at[:, lanes],
                sums,
                dq_t,
                dk_sum,
                dv_sum,
            )
            for n in range(*span):
                if ahead[n]:

                    @pl.when(i == n)
                    def _(events=ahead[n]):
                        emit_all(events)

            return carry

        lax.fori_loop(*span, body, 0)

    attend_loop(
        False,
        512,
        state_lengths_ref[me],
        pool.at[3],
        states.at[0],
        states.at[1],
        pool.at[4],
        (3, 4),
        2.0,
    )
    lse_load = pltpu.make_async_copy(lse_ref, lse_held, state_sem.at[3])
    lse_load.start()
    emit_all(planner.free_slot(9))
    weight_grad(9 % G_SLOTS, lambda: pool[1], columns_of(3))
    produced(9, 2.5)
    load(5, full_ref.at[4]).wait()
    load(6, o_ref).wait()
    product_nt(lambda: pool[3], rows_of(5), add_to_acc, turn_tile(1, 6))
    load(6, x_in_ref).start()
    load(5, full_ref.at[6]).start()
    load(3, q_ref).start()
    tick(2.5)
    states_t[...] = states[2].T
    for c, index in ((10, 0), (11, 1)):
        emit_all(planner.free_slot(c))
        weight_grad(
            c % G_SLOTS, lambda: states_t[...], lambda n, i=index: states[i, :, pl.ds(n, 256)]
        )
        produced(c, 1.0)
    load(7, full_ref.at[5]).wait()
    load(5, full_ref.at[6]).wait()

    def state_part(n):
        dims = (((1,), (1,)), ((), ()))
        return lax.dot_general(
            states[0], pool[7, pl.ds(n, 256), :], dims, preferred_element_type=jnp.float32
        ) + lax.dot_general(
            states[1], pool[5, pl.ds(n, 256), :], dims, preferred_element_type=jnp.float32
        )

    def put_state(i, carry):
        n = pl.multiple_of(i * 256, 256)
        state_grad_ref[:, pl.ds(n, 256)] = state_part(n).astype(jnp.bfloat16)
        return carry

    lax.fori_loop(0, 4, put_state, 0)
    load(5, k_ref).start()
    load(7, v_ref).start()
    tick(1.0)

    norm_back(r1_ref, 11, 11, 12, 2, 0)
    tick(4.0)
    emit_all(planner.free_slot(12))
    weight_grad(12 % G_SLOTS, lambda: pool[1], columns_of(0))
    produced(12, 2.5)
    load(2, full_ref.at[3]).wait()
    load(6, x_in_ref).wait()
    product_nt(lambda: pool[0], rows_of(2), put_in(4), turn_tile(1, 6))
    load(0, full_ref.at[0]).start()
    load(2, full_ref.at[1]).start()
    load(6, full_ref.at[2]).start()
    tick(2.5)
    load(3, q_ref).wait()
    load(5, k_ref).wait()
    load(7, v_ref).wait()
    lse_load.wait()
    def self_heads(span):
        refs = [pool.at[slot] for slot in (3, 5, 7, 4)]
        attend_loop(True, 256, lengths_ref[me], *refs, (0, 1), 5.0, span)

    def query_key_grad(c, half_of):
        def put(i, carry):
            n = pl.multiple_of((i % 2) * 256 + 512 * half_of, 256)
            value = product(pool[1], pool[3 + 2 * (i // 2), :, pl.ds(n, 256)])
            low = value.astype(jnp.bfloat16).reshape(4, 256, 256)
            made[c % G_SLOTS, :, :, pl.ds(pl.multiple_of(i * 256, 256), 256)] = low
            return carry

        emit_all(planner.free_slot(c))
        lax.fori_loop(0, 4, put, 0)
        produced(c, 2.5)

    self_heads((0, 4))
    query_key_grad(13, 0)
    self_heads((4, 8))

    def small_copy(k):
        source = small if k == 0 else small_sum.at[k - 1]
        device = (other_core, other_x, other_y)[k]
        return remote(source, small_in.at[k], small_send_sem.at[k], small_recv_sem.at[k], device)

    def small_z_copy(d):
        return remote(
            small_sum.at[2],
            small_z.at[z],
            small_send_sem.at[3 + d],
            small_recv_sem.at[3 + d],
            others_z[d],
        )

    def small_step(k):
        small_copy(k).wait()
        before = small[...] if k == 0 else small_sum[k - 1]
        small_sum[k] = before + small_in[k]
        if k < 2:
            small_copy(k + 1).start()
        else:
            small_z[z] = small_sum[2]
            for d in range(3):
                small_z_copy(d).start()

    small_copy(0).start()
    emit_all(planner.free_slot(14))
    weight_grad(14 % G_SLOTS, lambda: pool[1], columns_of(7))
    produced(14, 2.5)
    small_step(0)
    query_key_grad(15, 1)
    small_step(1)
    load(0, full_ref.at[0]).wait()
    product_nt(lambda: pool[3], rows_of(0), add_to_acc)
    tick(2.5)
    small_step(2)
    load(2, full_ref.at[1]).wait()
    product_nt(lambda: pool[5], rows_of(2), add_to_acc)
    tick(2.5)
    for d in range(3):
        small_z_copy(d).wait()
    totals_ref[...] = (small_z[0] + small_z[1]) + (small_z[2] + small_z[3])
    load(6, full_ref.at[2]).wait()

    def put_input(n, value):
        total = acc[:, pl.ds(n, 256)] + value
        pool[4, :, pl.ds(n, 256)] = total.astype(jnp.bfloat16)

    product_nt(lambda: pool[7], rows_of(6), put_input)
    token_copy = pltpu.make_async_copy(pool.at[4], token_grad_ref, load_sem.at[4])
    token_copy.start()
    tick(2.5)

    part[...] = jnp.zeros_like(part)

    def spot(place):
        return (0, 1, 2, 6)[place // 4], (place % 4) * 256

    def scan_load(place):
        slot, row = spot(place)
        return pltpu.make_async_copy(
            out_ref.at[place], pool.at[slot, pl.ds(row, 256), :], scan_sem.at[place]
        )

    scans = {}
    for i in range(2):
        scans[i] = ([(0, 512 * i, 512, i, 0), (2, 512 * i, 512, i, 512)], i, (13, 128 * i))
    for i in range(2, 8):
        scans[i] = ([(1 if i == 2 else i, 0, D, i, 0)], i, (13, 128 * i))
    scans[8] = ([(8 + i, 0, D, 8 + i, 0) for i in range(4)], 8, (14, 0))
    for i in range(4):
        scans[9 + i] = ([(12 + i, 0, D, 12, 0)], 9 + i, (14, 128))

    def scan(name):
        sources, row_lane, (total_row, total_lane) = scans[name]
        width = float(sum(source[2] for source in sources))
        step = 64 if name == 8 else 256

        def body(i, carry):
            cols, weights, total = carry
            r = pl.multiple_of(i * step, step)
            squares = []
            for place, lane, lanes, _, _ in sources:
                slot, row = spot(place)
                tile = pool[slot, pl.ds(row + r, step), lane : lane + lanes]
                squares.append(jnp.square(tile.astype(jnp.float32)))
            row_sum = sum(jnp.sum(square, axis=1, keepdims=True) for square in squares)
            rows = DECAY_RATE * rows_ref[pl.ds(r, step), row_lane : row_lane + 1] + (
                1.0 - DECAY_RATE
            ) * (row_sum / width + FACTOR_EPS)
            rows_out[pl.ds(r, step), row_lane : row_lane + 1] = rows
            inverse = 1.0 / rows
            cols = [c + fold(s) for c, s in zip(cols, squares)]
            weights = [w + fold(s * inverse) for w, s in zip(weights, squares)]
            return cols, weights, total + fold(rows)

        zeros = [jnp.zeros((8, source[2]), jnp.float32) for source in sources]
        cols, weights, total = lax.fori_loop(
            0, 256 // step, body, (zeros, zeros, jnp.zeros((8, 1), jnp.float32))
        )
        for (_, _, lanes, slot, lane), col, weighted in zip(sources, cols, weights):
            here = slice(lane, lane + lanes)
            part[slot : slot + 1, here] += jnp.sum(col, axis=0, keepdims=True)
            part[16 + slot : 17 + slot, here] += jnp.sum(weighted, axis=0, keepdims=True)
        part[total_row : total_row + 1, total_lane : total_lane + 128] += jnp.broadcast_to(
            jnp.sum(total), (1, 128)
        )

    chunk_at = {place: c for c, place in enumerate(place_of)}
    tasks = [
        ([chunk_at[source[0]] for source in scans[name][0]], name)
        for name in (9, 10, 11, 12, 8, 7, 4, 5, 6, 3, 2, 0, 1)
    ]
    loaded = set()
    for c in range(CHUNKS):
        if planner.stage[c] > 8:
            scan_load(place_of[c]).start()
    for first, second in planner.drain(tasks, 1.5):
        if first != "task":
            emit(first, second)
            if first == 8:
                scan_load(place_of[second]).start()
            continue
        for source in scans[second][0]:
            if source[0] not in loaded:
                loaded.add(source[0])
                scan_load(source[0]).wait()
        scan(second)
    total = line_sum(part, whole, line_send_sem, line_recv_sem, z, others_z)
    row_counts = [D] * 12 + [FF]
    means = [total[13:14, 128 * i : 128 * i + 1] / D for i in range(8)]
    means = means + [total[14:15, 0:1] / D] * 4 + [total[14:15, 128:129] / FF]
    cols_new, quotients = [], []
    for slot in range(13):
        new = DECAY_RATE * cols_ref[slot : slot + 1, :] + (1.0 - DECAY_RATE) * (
            total[slot : slot + 1] / row_counts[slot] + FACTOR_EPS
        )
        cols_new.append(new)
        quotients.append(jnp.sum(total[16 + slot : 17 + slot] / new, axis=1, keepdims=True))
        cols_out[slot : slot + 1, :] = new
    expand_quotient = quotients[8] + quotients[9] + quotients[10] + quotients[11]
    for slot in range(13):
        if slot < 8:
            mean_square = means[slot] * quotients[slot] / (D * D)
            rate = STEP_RATE * (OUT_GAIN if slot % 4 == 3 else 1.0)
        else:
            quotient = expand_quotient if slot < 12 else quotients[12]
            mean_square = means[slot] * quotient / (D * FF)
            rate = STEP_RATE
        factor = rate / jnp.maximum(1.0, jnp.sqrt(mean_square) / CLIP_LEVEL)
        scale_out[slot : slot + 1, :] = lax.rsqrt(cols_new[slot] / means[slot]) * factor
    token_copy.wait()


def backward(scalars, held, gains, small, factor_rows, factor_cols):
    any_space = pl.BlockSpec(memory_space=pl.ANY)
    vmem = pl.BlockSpec(memory_space=pltpu.VMEM)
    shape = jax.ShapeDtypeStruct
    dma = pltpu.SemaphoreType.DMA
    low = jnp.bfloat16
    wide = jnp.float32
    rows = small.shape[0]
    return pl.pallas_call(
        backward_kernel,
        out_shape=(
            shape((1024, D), low),
            shape((128, D), low),
            shape((CHUNKS, 256, D), low),
            shape(small.shape, wide),
            shape((256, 128), wide),
            shape((16, D), wide),
            shape((16, D), wide),
            shape((CHUNKS, 4, 128, D), low),
        ),
        in_specs=[SCALARS] * 2 + [any_space] * len(held) + [vmem] * 4,
        out_specs=(any_space, vmem, any_space, vmem, vmem, vmem, vmem, any_space),
        scratch_shapes=[
            pltpu.VMEM((POOL, 1024, D), low),
            pltpu.VMEM((1024, D), wide),
            pltpu.VMEM((G_SLOTS, 4, 256, D), low),
            pltpu.VMEM((R_SLOTS, 4, 128, D), low),
            pltpu.VMEM((CHUNKS, 4, 64, D), low),
            pltpu.VMEM((CHUNKS, 4, 32, D), low),
            pltpu.VMEM((CHUNKS, 3, 32, D), low),
            pltpu.VMEM((2, 128, D), wide),
            pltpu.VMEM((128, 1024), wide),
            pltpu.VMEM((2, 1024, 128), wide),
            pltpu.VMEM((2, 1024, 128), wide),
            pltpu.VMEM((8, 8, 1024), wide),
            pltpu.VMEM((3, 128, D), low),
            pltpu.VMEM((D, 128), low),
            pltpu.VMEM((rows, D), wide),
            pltpu.VMEM((3, rows, D), wide),
            pltpu.VMEM((3, rows, D), wide),
            pltpu.VMEM((4, rows, D), wide),
            pltpu.VMEM((32, D), wide),
            pltpu.VMEM((4, 32, D), wide),
            dma((POOL,)),
            dma((2,)),
            dma((4,)),
            dma((R_SLOTS,)),
            dma((CHUNKS,)),
            dma((3,)),
            dma((3,)),
            dma((6, CHUNKS)),
            dma((6, CHUNKS)),
            dma((CHUNKS, 3)),
            dma((CHUNKS, 3)),
            dma((CHUNKS,)),
            dma((6,)),
            dma((6,)),
        ],
        compiler_params=pltpu.CompilerParams(
            collective_id=0, has_side_effects=True, vmem_limit_bytes=62 * MIB
        ),
    )(*scalars, *held, gains, small, factor_rows, factor_cols)[0:7]


def line_sum(part, whole, send_sem, recv_sem, z, others_z):
    copies = [
        remote(part, whole.at[z], send_sem.at[d], recv_sem.at[d], others_z[d]) for d in range(3)
    ]
    for copy in copies:
        copy.start()
    whole[z] = part[...]
    for copy in copies:
        copy.wait()
    return (whole[0] + whole[1]) + (whole[2] + whole[3])


def update_attention_kernel(
    grad_ref, weight_ref, rows_ref, scale_ref, grad_out, new_out, copy_out, grads, change
):
    block = grad_ref.shape[1]
    for i in range(8):
        rows = lax.rsqrt(rows_ref[:, i : i + 1])
        every = pl.ds(i, block, stride=8)
        for lane in range(8):
            columns = slice(lane * 128, lane * 128 + 128)
            if i < 2:
                start = 512 * i + 128 * (lane % 4)
                grad = grad_ref[2 * (lane // 4), :, start : start + 128]
            else:
                grad = grad_ref[1 if i == 2 else i, :, columns]
            grad = grad.astype(jnp.float32)
            grads[lane, every, :] = grad
            change[lane, every, :] = grad * rows * scale_ref[i : i + 1, columns]
    for lane in range(8):
        columns = slice(lane * 128, lane * 128 + 128)
        grad_out[:, columns] = grads[lane]
        new = weight_ref[:, columns] - change[lane]
        new_out[:, columns] = new
        copy_out[:, columns] = new.astype(jnp.bfloat16)


def update_attention(grads, weights, rows, scale):
    block = 64
    wide = pl.BlockSpec((block * 8, D), lambda i: (i, 0))
    shape = jax.ShapeDtypeStruct
    new = pl.pallas_call(
        update_attention_kernel,
        grid=(256 // block,),
        out_shape=(
            shape((2048, D), jnp.float32),
            shape((2048, D), jnp.float32),
            shape((2048, D), jnp.bfloat16),
        ),
        in_specs=[
            pl.BlockSpec((8, block, D), lambda i: (0, i, 0)),
            wide,
            pl.BlockSpec((block, 128), lambda i: (i, 0)),
            pl.BlockSpec((16, D), lambda i: (0, 0)),
        ],
        out_specs=(wide,) * 3,
        scratch_shapes=[pltpu.VMEM((8, block * 8, 128), jnp.float32)] * 2,
        compiler_params=pltpu.CompilerParams(vmem_limit_bytes=62 * MIB),
    )(grads, weights.reshape(2048, D), rows, scale)
    return [t.reshape(256, 8, D) for t in new]


def update_kernel(
    first, slots, grad_ref, weight_ref, rows_ref, scale_ref, grad_out, new_out, copy_out
):
    spans = 4 if slots == 4 else 1
    wide = D // spans
    for i in range(slots):
        grads = grad_ref[i].astype(jnp.float32)
        changes = grads * (lax.rsqrt(rows_ref[...]) * scale_ref[first + i : first + i + 1, :])
        for s in range(spans):
            start = s * D + i * wide
            columns = slice(start, start + wide)
            part = slice(s * wide, s * wide + wide)
            grad_out[:, columns] = grads[:, part]
            new = weight_ref[:, columns] - changes[:, part]
            new_out[:, columns] = new
            copy_out[:, columns] = new.astype(jnp.bfloat16)


def update_plain(grads, weights, rows, scale, first, slots, grad_map):
    count, width = weights.shape
    block = 256 // slots
    wide = pl.BlockSpec((block, width), lambda i: (i, 0))
    shape = jax.ShapeDtypeStruct
    return pl.pallas_call(
        lambda *refs: update_kernel(first, slots, *refs),
        grid=(count // block,),
        out_shape=(
            shape(weights.shape, jnp.float32),
            shape(weights.shape, jnp.float32),
            shape(weights.shape, jnp.bfloat16),
        ),
        in_specs=[
            pl.BlockSpec((slots, block, D), grad_map),
            wide,
            pl.BlockSpec((block, 1), lambda i: (i, 0)),
            pl.BlockSpec((16, D), lambda i: (0, 0)),
        ],
        out_specs=(wide,) * 3,
        compiler_params=pltpu.CompilerParams(vmem_limit_bytes=62 * MIB),
    )(grads, weights, rows, scale)


def update_direct(grads, rows, scale, attention_weights, expand_weight, shrink_weight):
    shr_rows = rows[:, 9:13].T.reshape(-1, 1)
    attention = update_attention(grads, attention_weights, rows, scale)
    expand = update_plain(grads, expand_weight, rows[:, 8:9], scale, 8, 4, lambda i: (2, i, 0))
    shrink = update_plain(
        grads, shrink_weight, shr_rows, scale, 12, 1, lambda i: (12 + i, 0, 0)
    )
    return attention, expand, shrink, (rows[:, 0:8].T, rows[:, 8], shr_rows[:, 0])


def as_rows(vector):
    rows = -(-vector.shape[0] // 1024) * 8
    return jnp.pad(vector, (0, rows * 128 - vector.shape[0])).reshape(rows, 128)


def masked_scores(query_part, key_heads, first_row, valid_count, causal):
    scores = jnp.einsum("qhd,khd->hqk", query_part, key_heads, preferred_element_type=jnp.float32)
    key_places = jnp.arange(key_heads.shape[0], dtype=jnp.int32)[None, :]
    usable = key_places < valid_count
    if causal:
        query_places = first_row + jnp.arange(query_part.shape[0], dtype=jnp.int32)[:, None]
        usable = usable & (key_places <= query_places)
    return jnp.where(usable[None], scores, MASKED)


def attend_forward(queries, key_heads, values, valid_count, causal):
    query_rows = queries.shape[0]
    step_rows = min(512, query_rows)
    outputs, stored = ([], [])
    for b in range(query_rows // step_rows):
        first_row = b * step_rows
        key_end = first_row + step_rows if causal else key_heads.shape[0]
        scores = masked_scores(
            queries[first_row : first_row + step_rows],
            key_heads[:key_end],
            first_row,
            valid_count,
            causal,
        )
        row_max = jnp.max(scores, axis=-1, keepdims=True)
        raised = jnp.exp(scores - row_max)
        totals = jnp.sum(raised, axis=-1, keepdims=True)
        probs_low = (raised / totals).astype(jnp.bfloat16)
        outputs.append(
            jnp.einsum(
                "hqk,khd->qhd", probs_low, values[:key_end], preferred_element_type=jnp.float32
            )
        )
        stored.append(row_max + jnp.log(totals))
    return (jnp.concatenate(outputs, axis=0), stored)


def attend_backward(queries, key_heads, values, grad_out, stored, valid_count, causal):
    query_rows = queries.shape[0]
    key_rows = key_heads.shape[0]
    step_rows = min(512, query_rows)
    grad_queries = []
    grad_keys = jnp.zeros(key_heads.shape, jnp.float32)
    grad_values = jnp.zeros(values.shape, jnp.float32)
    for b in range(query_rows // step_rows):
        first_row = b * step_rows
        key_end = first_row + step_rows if causal else key_rows
        query_part = queries[first_row : first_row + step_rows]
        grad_part = grad_out[first_row : first_row + step_rows]
        scores = masked_scores(query_part, key_heads[:key_end], first_row, valid_count, causal)
        probs = jnp.exp(scores - stored[b])
        probs_low = probs.astype(jnp.bfloat16)
        grad_probs = jnp.einsum(
            "qhd,khd->hqk", grad_part, values[:key_end], preferred_element_type=jnp.float32
        )
        value_part = jnp.einsum(
            "hqk,qhd->khd", probs_low, grad_part, preferred_element_type=jnp.float32
        )
        grad_scores = probs * (grad_probs - jnp.sum(probs * grad_probs, axis=-1, keepdims=True))
        scores_low = grad_scores.astype(jnp.bfloat16)
        grad_queries.append(
            jnp.einsum(
                "hqk,khd->qhd", scores_low, key_heads[:key_end], preferred_element_type=jnp.float32
            )
        )
        key_part = jnp.einsum(
            "hqk,qhd->khd", scores_low, query_part, preferred_element_type=jnp.float32
        )
        padding = ((0, key_rows - key_end), (0, 0), (0, 0))
        grad_keys = grad_keys + jnp.pad(key_part, padding)
        grad_values = grad_values + jnp.pad(value_part, padding)
    return (jnp.concatenate(grad_queries, axis=0), grad_keys, grad_values)


def gather_rows(piece):
    return lax.all_gather(piece, ("shard", "rep"), axis=0, tiled=True)


def own_piece(block, replicas):
    rows = block.shape[0] // replicas
    return lax.dynamic_slice_in_dim(block, lax.axis_index("rep") * rows, rows, axis=0)


def scatter_rows(grad):
    piece = lax.psum_scatter(
        grad.astype(jnp.bfloat16), ("shard", "rep"), scatter_dimension=0, tiled=True
    )
    return lax.all_gather(piece, "rep", axis=0, tiled=True)


def local_factors(grad, rows):
    square = grad * grad
    rows_new = DECAY_RATE * rows + (1.0 - DECAY_RATE) * jnp.mean(square + FACTOR_EPS, axis=-1)
    col_part = jnp.sum(square + FACTOR_EPS, axis=0)
    weighted = jnp.sum(square / rows_new[..., None], axis=0)
    return rows_new, col_part, weighted, jnp.sum(rows_new, axis=0)


def finish_factors(grad, weight, rows_new, cols, col_sum, weighted, row_total, row_count, rate):
    cols_new = DECAY_RATE * cols + (1.0 - DECAY_RATE) * col_sum / row_count
    mean_rows = row_total / row_count
    mean_square = mean_rows * jnp.sum(weighted / cols_new, axis=-1) / (row_count * cols.shape[-1])
    factor = rate / jnp.maximum(1.0, jnp.sqrt(mean_square) / CLIP_LEVEL)
    scaled = lax.rsqrt(cols_new / mean_rows[..., None]) * factor[..., None]
    fresh = weight - grad * (lax.rsqrt(rows_new)[..., None] * scaled[None])
    return fresh, cols_new


def plain_device(
    tokens,
    encoder,
    cotangent,
    lengths,
    encoder_lengths,
    dealt_order,
    attention_weights,
    expand_weight,
    shrink_weight,
    small_params,
    attention_rows,
    attention_cols,
    expand_rows,
    expand_cols,
    shrink_rows,
    shrink_cols,
    small_moment,
):
    devices = lax.axis_size(("rep", "shard"))
    replicas = lax.axis_size("rep")
    shards = lax.axis_size("shard")
    slot_tokens = tokens.shape[0]
    slot_states = encoder.shape[0]
    position = lax.axis_index(("rep", "shard"))
    inverse = (
        jnp.zeros((devices,), jnp.int32).at[dealt_order].set(jnp.arange(devices, dtype=jnp.int32))
    )
    qkv_piece = own_piece(attention_weights[:, 0:3, :].reshape(-1, 3 * D), replicas)
    rest_piece = own_piece(attention_weights[:, 3:8, :].reshape(-1, 5 * D), replicas)
    qkv_full = gather_rows(qkv_piece.astype(jnp.bfloat16))
    rest_full = gather_rows(rest_piece.astype(jnp.bfloat16))
    expand_full = gather_rows(own_piece(expand_weight, replicas).astype(jnp.bfloat16))
    shrink_full = gather_rows(own_piece(shrink_weight, replicas).astype(jnp.bfloat16))
    spread = lax.all_to_all(
        tokens.reshape(devices, slot_tokens // devices, D),
        ("rep", "shard"),
        split_axis=0,
        concat_axis=0,
        tiled=True,
    )
    picked = jnp.take(spread, inverse, axis=0)
    tokens = lax.all_to_all(
        picked, ("rep", "shard"), split_axis=0, concat_axis=0, tiled=True
    ).reshape(slot_tokens, D)
    states = encoder
    incoming = cotangent
    valid_tokens = lengths[position]
    valid_states = encoder_lengths[position]
    matrices = [qkv_full[:, i * D : (i + 1) * D] for i in range(3)] + [
        rest_full[:, i * D : (i + 1) * D] for i in range(5)
    ]
    parts = unpack(small_params)
    token_heads = (slot_tokens, HEADS, HEAD_DIM)
    state_heads = (slot_states, HEADS, HEAD_DIM)
    q_self = ((forward_product(tokens, matrices[0]) + parts[0]) * 0.125).astype(
        jnp.bfloat16
    )
    k_self = forward_product(tokens, matrices[1]).astype(jnp.bfloat16)
    v_self = (forward_product(tokens, matrices[2]) + parts[1]).astype(jnp.bfloat16)
    o_self, lse_self = attend_forward(
        q_self.reshape(token_heads),
        k_self.reshape(token_heads),
        v_self.reshape(token_heads),
        valid_tokens,
        True,
    )
    o_self_low = o_self.reshape(slot_tokens, D).astype(jnp.bfloat16)
    branch_a = forward_product(o_self_low, matrices[3]) + parts[2]
    tokens_wide = tokens.astype(jnp.float32)
    hidden_one, norm_one_back = jax.vjp(layer_norm, tokens_wide + branch_a, parts[8], parts[9])
    hidden_one_low = hidden_one.astype(jnp.bfloat16)
    q_cross = (
        (forward_product(hidden_one_low, matrices[4]) + parts[3]) * 0.125
    ).astype(jnp.bfloat16)
    k_cross = forward_product(states, matrices[5]).astype(jnp.bfloat16)
    v_cross = (forward_product(states, matrices[6]) + parts[4]).astype(jnp.bfloat16)
    o_cross, lse_cross = attend_forward(
        q_cross.reshape(token_heads),
        k_cross.reshape(state_heads),
        v_cross.reshape(state_heads),
        valid_states,
        False,
    )
    o_cross_low = o_cross.reshape(slot_tokens, D).astype(jnp.bfloat16)
    branch_c = forward_product(o_cross_low, matrices[7]) + parts[5]
    hidden_two, norm_two_back = jax.vjp(layer_norm, hidden_one + branch_c, parts[10], parts[11])
    hidden_two_low = hidden_two.astype(jnp.bfloat16)
    pre_act = forward_product(hidden_two_low, expand_full) + parts[6]
    activated, gelu_back = jax.vjp(gelu_exact, pre_act)
    activated_low = activated.astype(jnp.bfloat16)
    branch_m = forward_product(activated_low, shrink_full) + parts[7]
    result, norm_three_back = jax.vjp(layer_norm, hidden_two + branch_m, parts[12], parts[13])
    usable_rows = (jnp.arange(slot_tokens, dtype=jnp.int32) < valid_tokens).astype(jnp.float32)[
        :, None
    ]
    squares = jnp.stack(
        [
            jnp.sum(usable_rows * t * t)
            for t in (tokens_wide, branch_a, hidden_one, branch_c, hidden_two, branch_m)
        ]
    )
    d_third, d_gain_three, d_shift_three = norm_three_back(
        incoming.astype(jnp.float32) * usable_rows
    )
    d_mlp = d_third.astype(jnp.bfloat16)
    grad_shrink = weight_product(activated_low, d_mlp)
    grad_shrink_offset = row_sum(d_mlp)
    d_activated = input_product(d_mlp, shrink_full)
    d_pre = gelu_back(d_activated)[0].astype(jnp.bfloat16)
    grad_expand = weight_product(hidden_two_low, d_pre)
    grad_expand_offset = row_sum(d_pre)
    d_hidden_two = d_third + input_product(d_pre, expand_full)
    d_second, d_gain_two, d_shift_two = norm_two_back(d_hidden_two)
    d_branch_c = d_second.astype(jnp.bfloat16)
    grad_cross_out = weight_product(o_cross_low, d_branch_c)
    grad_cross_out_offset = row_sum(d_branch_c)
    d_o_cross = input_product(d_branch_c, matrices[7]).astype(jnp.bfloat16)
    grad_cq, grad_ck, grad_cv = attend_backward(
        q_cross.reshape(token_heads),
        k_cross.reshape(state_heads),
        v_cross.reshape(state_heads),
        d_o_cross.reshape(token_heads),
        lse_cross,
        valid_states,
        False,
    )
    dq_cross = (grad_cq.reshape(slot_tokens, D) * 0.125).astype(jnp.bfloat16)
    dk_cross = grad_ck.reshape(slot_states, D).astype(jnp.bfloat16)
    dv_cross = grad_cv.reshape(slot_states, D).astype(jnp.bfloat16)
    grad_cross_query = weight_product(hidden_one_low, dq_cross)
    grad_cross_key = weight_product(states, dk_cross)
    grad_cross_value = weight_product(states, dv_cross)
    state_grad = input_product(dk_cross, matrices[5]) + input_product(
        dv_cross, matrices[6]
    )
    d_hidden_one = d_second + input_product(dq_cross, matrices[4])
    d_first, d_gain_one, d_shift_one = norm_one_back(d_hidden_one)
    d_branch_a = d_first.astype(jnp.bfloat16)
    grad_self_out = weight_product(o_self_low, d_branch_a)
    grad_self_out_offset = row_sum(d_branch_a)
    d_o_self = input_product(d_branch_a, matrices[3]).astype(jnp.bfloat16)
    grad_sq, grad_sk, grad_sv = attend_backward(
        q_self.reshape(token_heads),
        k_self.reshape(token_heads),
        v_self.reshape(token_heads),
        d_o_self.reshape(token_heads),
        lse_self,
        valid_tokens,
        True,
    )
    dq_self = (grad_sq.reshape(slot_tokens, D) * 0.125).astype(jnp.bfloat16)
    dk_self = grad_sk.reshape(slot_tokens, D).astype(jnp.bfloat16)
    dv_self = grad_sv.reshape(slot_tokens, D).astype(jnp.bfloat16)
    grad_self_query = weight_product(tokens, dq_self)
    grad_self_key = weight_product(tokens, dk_self)
    grad_self_value = weight_product(tokens, dv_self)
    token_grad = (
        d_first
        + input_product(dq_self, matrices[0])
        + input_product(dk_self, matrices[1])
        + input_product(dv_self, matrices[2])
    )
    small_partial = jnp.concatenate(
        [
            row_sum(dq_self),
            row_sum(dv_self),
            grad_self_out_offset,
            row_sum(dq_cross),
            row_sum(dv_cross),
            grad_cross_out_offset,
            grad_expand_offset,
            grad_shrink_offset,
            d_gain_one,
            d_shift_one,
            d_gain_two,
            d_shift_two,
            d_gain_three,
            d_shift_three,
        ]
    )
    totals = lax.psum(jnp.concatenate([small_partial, squares]), ("rep", "shard"))
    g_shrink = scatter_rows(grad_shrink)
    g_expand = scatter_rows(grad_expand)
    g_rest = scatter_rows(
        jnp.concatenate(
            [grad_self_out, grad_cross_query, grad_cross_key, grad_cross_value, grad_cross_out],
            axis=1,
        )
    )
    g_qkv = scatter_rows(
        jnp.concatenate([grad_self_query, grad_self_key, grad_self_value], axis=1)
    )
    g_attention = (
        jnp.concatenate([g_qkv, g_rest], axis=1).reshape(-1, 8, D).astype(jnp.float32)
    )
    g_expand = g_expand.astype(jnp.float32)
    g_shrink = g_shrink.astype(jnp.float32)
    attention_rows_new, *attention_parts = local_factors(g_attention, attention_rows.T)
    expand_rows_new, *expand_parts = local_factors(g_expand, expand_rows)
    shrink_rows_new, *shrink_parts = local_factors(g_shrink, shrink_rows)
    flat = attention_parts + expand_parts + shrink_parts
    summed = lax.psum(jnp.concatenate([t.reshape(-1) for t in flat]), "shard")
    sums = []
    offset = 0
    for t in flat:
        sums.append(summed[offset : offset + t.size].reshape(t.shape))
        offset = offset + t.size
    attention_rates = STEP_RATE * jnp.where(jnp.arange(8) % 4 == 3, OUT_GAIN, 1.0).astype(
        jnp.float32
    )
    attention_new, attention_cols_new = finish_factors(
        g_attention,
        attention_weights,
        attention_rows_new,
        attention_cols,
        *sums[0:3],
        D,
        attention_rates,
    )
    expand_new, expand_cols_new = finish_factors(
        g_expand, expand_weight, expand_rows_new, expand_cols, *sums[3:6], D, STEP_RATE
    )
    shrink_new, shrink_cols_new = finish_factors(
        g_shrink, shrink_weight, shrink_rows_new, shrink_cols, *sums[6:9], FF, STEP_RATE
    )
    small_grad = totals[: small_params.shape[0]]
    small_moment_new = DECAY_RATE * small_moment + (1.0 - DECAY_RATE) * (
        small_grad * small_grad + FACTOR_EPS
    )
    small_update = small_grad * lax.rsqrt(small_moment_new)
    small_scale = jnp.sqrt(jnp.mean(small_update * small_update))
    small_new = small_params - SMALL_RATE * small_update / jnp.maximum(
        1.0, small_scale / CLIP_LEVEL
    )
    norm_stats = jnp.sqrt(
        totals[small_params.shape[0] :] / (jnp.sum(lengths).astype(jnp.float32) * D)
    )
    return (
        result.astype(jnp.bfloat16),
        token_grad.astype(jnp.bfloat16),
        state_grad.astype(jnp.bfloat16),
        g_attention,
        g_expand,
        g_shrink,
        small_grad,
        attention_new,
        expand_new,
        shrink_new,
        small_new,
        attention_new.astype(jnp.bfloat16),
        expand_new.astype(jnp.bfloat16),
        shrink_new.astype(jnp.bfloat16),
        attention_rows_new.T,
        attention_cols_new,
        expand_rows_new,
        expand_cols_new,
        shrink_rows_new,
        shrink_cols_new,
        small_moment_new,
        norm_stats,
    )


def direct_device(
    tokens,
    encoder,
    cotangent,
    lengths,
    encoder_lengths,
    dealt_order,
    attention_weights,
    expand_weight,
    shrink_weight,
    small_params,
    attention_rows,
    attention_cols,
    expand_rows,
    expand_cols,
    shrink_rows,
    shrink_cols,
    small_moment,
):
    inverse = jnp.zeros((32,), jnp.int32).at[dealt_order].set(jnp.arange(32, dtype=jnp.int32))
    params = small_params.reshape(17, D)
    weights = (attention_weights.reshape(2048, D), expand_weight, shrink_weight)
    (
        tokens,
        full,
        q_self,
        k_self,
        v_self,
        o_self,
        lse_self,
        q_cross,
        k_cross,
        v_cross,
        o_cross,
        lse_cross,
        summed_one,
        summed_two,
        hidden_one,
        hidden_two,
        activated,
        slope,
        output,
        d_mlp,
        d_third,
        small_first,
    ) = forward(
        (inverse, lengths, encoder_lengths), tokens, weights, encoder, cotangent, params
    )
    factor_rows = jnp.concatenate(
        [attention_rows, expand_rows.reshape(1, 256), shrink_rows.reshape(4, 256)]
    )
    factor_rows = jnp.pad(factor_rows.T, ((0, 0), (0, 115)))
    factor_cols = jnp.concatenate(
        [attention_cols, hidden_blocks(expand_cols), shrink_cols.reshape(1, D), jnp.ones((3, D))]
    )
    token_grad, state_grad, reduced, totals, factor_rows, factor_cols, scale = backward(
        (lengths, encoder_lengths),
        (
            d_mlp,
            d_third,
            activated,
            slope,
            full.reshape(GATHERED, 1024, D),
            hidden_two,
            hidden_one,
            tokens.reshape(1024, D),
            encoder,
            o_cross,
            o_self,
            summed_one,
            summed_two,
            q_self,
            k_self,
            v_self,
            q_cross,
            k_cross,
            v_cross,
            lse_self,
            lse_cross,
        ),
        params,
        small_first,
        factor_rows,
        factor_cols,
    )
    attention, expand, shrink, rows_new = update_direct(
        reduced, factor_rows, scale, attention_weights, expand_weight, shrink_weight
    )
    cols_new = (factor_cols[0:8], hidden_flat(factor_cols[8:12]), factor_cols[12])
    small_grad = totals[0:17].reshape(-1)
    small_moment_new = DECAY_RATE * small_moment + (1.0 - DECAY_RATE) * (
        small_grad * small_grad + FACTOR_EPS
    )
    small_update = small_grad * lax.rsqrt(small_moment_new)
    small_scale = jnp.sqrt(jnp.mean(small_update * small_update))
    small_new = small_params - SMALL_RATE * small_update / jnp.maximum(
        1.0, small_scale / CLIP_LEVEL
    )
    norm_stats = jnp.sqrt(totals[17, 0:6] / (jnp.sum(lengths).astype(jnp.float32) * D))
    return (
        output,
        token_grad,
        state_grad,
        attention[0],
        expand[0],
        shrink[0],
        small_grad,
        attention[1],
        expand[1],
        shrink[1],
        small_new,
        attention[2],
        expand[2],
        shrink[2],
        rows_new[0],
        cols_new[0],
        rows_new[1],
        cols_new[1],
        rows_new[2],
        cols_new[2],
        small_moment_new,
        norm_stats,
    )


def on_device(*args):
    if lax.axis_size("rep") == 8 and lax.axis_size("shard") == 4:
        return direct_device(*args)
    return plain_device(*args)


def solution(mesh):
    in_specs = (
        P(("rep", "shard"), None),
        P(("rep", "shard"), None),
        P(("rep", "shard"), None),
        P(),
        P(),
        P(),
        P("shard", None, None),
        P("shard", None),
        P("shard", None),
        P(),
        P(None, "shard"),
        P(),
        P("shard"),
        P(),
        P("shard"),
        P(),
        P(),
    )
    out_specs = (
        P(("rep", "shard"), None),
        P(("rep", "shard"), None),
        P(("rep", "shard"), None),
        P("shard", None, None),
        P("shard", None),
        P("shard", None),
        P(),
        P("shard", None, None),
        P("shard", None),
        P("shard", None),
        P(),
        P("shard", None, None),
        P("shard", None),
        P("shard", None),
        P(None, "shard"),
        P(),
        P("shard"),
        P(),
        P("shard"),
        P(),
        P(),
        P(),
    )
    return jax.shard_map(
        on_device, mesh=mesh, in_specs=in_specs, out_specs=out_specs, check_vma=False
    )
```

profile of v0, /device:TPU:16, one launch (start us, length us, event | category | flops | bytes accessed | tf_op | source)
XLA Modules:
  0.0 582.0 jit_solution(9231264224977504469)
XLA Ops:
  0.7 0.7 compare_select_fusion
  1.3 1.2 scatter_custom_fusion.order_ref
  2.5 1.5 reshape.101.par.gains_ref
  4.0 0.0 copy-start.9
  4.0 0.0 copy-start.13
  4.1 282.9 %shard_map.336 = (bf16[32,32,1024]{2,1,0:T(8,128)(2,1)}, bf16[16,4,256,1024]{3,2,1,0:T(8,128)(2,1)}, bf16[1024,1024]{1,0:T(8,128)(2,1)}, bf16[1024,1024]{1,0:T(8...) custom-call(s32[32]{0:T(128)} %scatter_custom_fusion.order_ref, ...), custom_call_target="tpu_custom_call" | custom-call | tf_op jit(solution)/shard_map/pallas_call | solution.py:900
  287.0 0.0 copy-done.12
  287.0 0.0 copy-done.11
  287.0 0.0 copy-done.15
  287.1 0.1 copy.50
  287.2 0.7 pad.4.rows_ref
  287.9 0.0 copy-done.10
  287.9 0.1 pad.8.clone
  288.0 0.0 copy-done.9
  288.0 0.0 copy-done.13
  288.0 0.7 maximum_maximum_fusion.cols_ref
  288.7 248.7 %shard_map.337 = (bf16[1024,1024]{1,0:T(8,128)(2,1)}, bf16[128,1024]{1,0:T(8,128)(2,1)}, bf16[16,256,1024]{2,1,0:T(8,128)(2,1)}, f32[24,1024]{1,0:T(8,128)}, f32...) custom-call(s32[32]{0:T(128)} %lengths_ref.3, ...), custom_call_target="tpu_custom_call" | custom-call | tf_op jit(solution)/shard_map/pallas_call | solution.py:1794
  537.3 0.0 copy-start
  537.3 14.7 %shard_map.338 = (f32[2048,1024]{1,0:T(8,128)}, f32[2048,1024]{1,0:T(8,128)}, bf16[2048,1024]{1,0:T(8,128)(2,1)}) custom-call(bf16[16,256,1024]{2,1,0:T(8,128)(2,1)} %get-tuple-element.84.grad_ref.refs_0_, f32[2048,1024]{1,0:T(8,128)} %bitcast.33, f32[256,128]{1,0:T(8,128)} %get-tuple-element.85.rows_ref, f32[16,1024]{1,0:T(8,128)} %get-tuple-element.86.scale_ref.refs_3_), custom_call_target="tpu_custom_call" | custom-call | tf_op jit(solution)/shard_map/pallas_call | solution.py:1891
  552.0 0.0 copy-done
  552.1 1.3 slice_reduce_fusion
  553.4 7.2 %shard_map.339 = (f32[256,4096]{1,0:T(8,128)}, f32[256,4096]{1,0:T(8,128)}, bf16[256,4096]{1,0:T(8,128)(2,1)}) custom-call(bf16[16,256,1024]{2,1,0:T(8,128)(2,1)} %get-tuple-element.84.grad_ref.refs_0_, f32[256,4096]{1,0:T(8,128)} %refs_1_.2, f32[256,1]{1,0:T(8,128)} %get-tuple-element.167.refs_2_, f32[16,1024]{1,0:T(8,128)} %get-tuple-element.86.scale_ref.refs_3_), custom_call_target="tpu_custom_call" | custom-call | tf_op jit(solution)/shard_map/pallas_call | solution.py:1935
  560.6 0.1 slice_bitcast_fusion.1
  560.7 0.1 copy.51
  560.8 1.0 copy.57
  561.8 0.0 copy-start.14
  561.8 7.5 %shard_map.340 = (f32[1024,1024]{1,0:T(8,128)}, f32[1024,1024]{1,0:T(8,128)}, bf16[1024,1024]{1,0:T(8,128)(2,1)}) custom-call(bf16[16,256,1024]{2,1,0:T(8,128)(2,1)} %get-tuple-element.84.grad_ref.refs_0_, f32[1024,1024]{1,0:T(8,128)} %refs_1_.3, f32[1024,1]{1,0:T(8,128)} %bitcast.37, f32[16,1024]{1,0:T(8,128)} %get-tuple-element.86.scale_ref.refs_3_), custom_call_target="tpu_custom_call" | custom-call | tf_op jit(solution)/shard_map/pallas_call | solution.py:1935
  569.4 0.0 copy-done.6
  569.4 0.0 copy-start.2
  569.4 0.0 copy-done.7
  569.4 0.6 multiply_reduce_fusion
  570.8 0.0 copy-done.3
  570.8 0.7 divide_subtract_fusion
  571.4 0.0 copy-start.1
  571.4 0.7 copy.55
  572.1 0.0 copy-done.8
  572.1 0.6 slice.29
  572.7 0.6 copy.58
  573.4 0.6 copy.59
  574.0 0.6 slice.31
  574.6 0.0 copy-done.14
  574.6 0.6 reduce_sum.19
  575.8 0.5 sqrt_bitcast_fusion
  576.4 3.1 copy.63
  579.5 0.0 copy-done.1
  579.5 1.3 copy.64
  580.8 0.0 copy-done.2
  580.8 0.7 copy.65
  (21 shorter events, 0.1 us)
Async XLA Ops:
  4.0 283.0 %copy-start.12 = (f32[1024]{0:T(1024)S(1)}, f32[1024]{0:T(1024)}, u32[]{:S(2)}) copy-start(f32[1024]{0:T(1024)} %param.31) | copy-start | bytes 12292
  4.0 283.0 %copy-start.11 = (f32[8,256]{1,0:T(8,128)S(1)}, f32[8,256]{1,0:T(8,128)}, u32[]{:S(2)}) copy-start(f32[8,256]{1,0:T(8,128)} %param.27) | copy-start | bytes 24580
  4.0 283.0 %copy-start.15 = (f32[256]{0:T(256)S(1)}, f32[256]{0:T(256)}, u32[]{:S(2)}) copy-start(f32[256]{0:T(256)} %param.29) | copy-start | bytes 3076
  4.0 283.8 %copy-start.10 = (f32[4096]{0:T(1024)S(1)}, f32[4096]{0:T(1024)}, u32[]{:S(2)}) copy-start(f32[4096]{0:T(1024)} %param.30) | copy-start | bytes 49156
  4.0 283.9 %copy-start.9 = (f32[8,1024]{1,0:T(8,128)S(1)}, f32[8,1024]{1,0:T(8,128)}, u32[]{:S(2)}) copy-start(f32[8,1024]{1,0:T(8,128)} %param.28) | copy-start | bytes 98308
  4.0 283.9 %copy-start.13 = (f32[1024]{0:T(1024)S(1)}, f32[1024]{0:T(1024)}, u32[]{:S(2)}) copy-start(f32[1024]{0:T(1024)} %param.32) | copy-start | bytes 12292
  537.3 14.7 %copy-start = (f32[256,128]{1,0:T(8,128)S(1)}, f32[256,128]{1,0:T(8,128)}, u32[]{:S(2)}) copy-start(f32[256,128]{1,0:T(8,128)} %get-tuple-element.85.rows_ref) | copy-start | bytes 393220
  561.8 7.6 %copy-start.6 = (f32[24,1024]{1,0:T(8,128)S(1)}, f32[24,1024]{1,0:T(8,128)}, u32[]{:S(2)}) copy-start(f32[24,1024]{1,0:T(8,128)} %get-tuple-element.90) | copy-start | bytes 294916
  561.8 7.6 %copy-start.7 = (f32[17408]{0:T(1024)S(1)}, f32[17408]{0:T(1024)}, u32[]{:S(2)}) copy-start(f32[17408]{0:T(1024)} %param.33) | copy-start | bytes 208900
  561.8 8.9 %copy-start.3 = (f32[17408]{0:T(1024)S(1)}, f32[17408]{0:T(1024)}, u32[]{:S(2)}) copy-start(f32[17408]{0:T(1024)} %param.26) | copy-start | bytes 208900
  561.8 10.3 %copy-start.8 = (f32[16,1024]{1,0:T(8,128)S(1)}, f32[16,1024]{1,0:T(8,128)}, u32[]{:S(2)}) copy-start(f32[16,1024]{1,0:T(8,128)} %get-tuple-element.97) | copy-start | bytes 196612
  561.8 12.7 %copy-start.14 = (s32[32]{0:T(128)S(1)}, s32[32]{0:T(128)}, u32[]{:S(2)}) copy-start(s32[32]{0:T(128)} %lengths_ref.3) | copy-start | bytes 388
  569.4 11.4 %copy-start.2 = (f32[17408]{0:T(1024)}, f32[17408]{0:T(1024)S(1)}, u32[]{:S(2)}) copy-start(f32[17408]{0:T(1024)S(1)} %reshape.111) | copy-start | bytes 208900
  570.1 10.8 %copy-start.4 = (f32[17408]{0:T(1024)}, f32[17408]{0:T(1024)S(1)}, u32[]{:S(2)}) copy-start(f32[17408]{0:T(1024)S(1)} %get-tuple-element.210) | copy-start | bytes 208900
  571.4 8.1 %copy-start.1 = (bf16[1024,1024]{1,0:T(8,128)(2,1)S(1)}, bf16[1024,1024]{1,0:T(8,128)(2,1)}, u32[]{:S(2)}) copy-start(bf16[1024,1024]{1,0:T(8,128)(2,1)} %get-tuple-element.191) | copy-start | bytes 6291460
  576.4 4.5 copy-start.5
where the time goes:
time: 591 us; the launch traced here: 582 us
  Pallas kernels  561 us (95%)
  local copies, waits for them, and re-layouts  14.5 us (2%)
    pallas_call x1, Pallas kernels, forward(): pl.pallas_call(forward_kernel, out_shape=outs, in_specs=[SCALARS] * 3 + [...  283 us
    pallas_call x1, Pallas kernels, backward(): pl.pallas_call(backward_kernel, out_shape=(shape((1024, D), low), shape((...  249 us
    pallas_call x2, Pallas kernels, update_plain(): pl.pallas_call(lambda *refs: update_kernel(first, slots, *refs), grid=(co...  14.8 us
    pallas_call x1, Pallas kernels, update_attention(): pl.pallas_call(update_attention_kernel, grid=(256 // block,), out_shape=(...  14.7 us

commit v1 on v0

--- a/solution.py
+++ b/solution.py
@@ -655,9 +655,11 @@
     small_out[...] = jnp.zeros_like(small_out)
     turn_back()
     planner.spend(56.0, z=42.0, x=21.0, y=21.0)
-    planner.opened = 5
+    planner.opened = 6
     for i in range(3):
         weight(i, 1 + i).start()
+    tick(20.0)
+    tick(8.0)
     own_back().wait()
     each_other(lambda offset: back_copy(offset).wait())
     planner.spend(112.0)

time: 591 us -> 595 us (level)
  no operation moved by 1% of the time
where the time goes in v1:
time: 595 us; the launch traced here: 587 us
  Pallas kernels  566 us (95%)
  local copies, waits for them, and re-layouts  14.5 us (2%)
    pallas_call x1, Pallas kernels, forward(): pl.pallas_call(forward_kernel, out_shape=outs, in_specs=[SCALARS] * 3 + [...  285 us
    pallas_call x1, Pallas kernels, backward(): pl.pallas_call(backward_kernel, out_shape=(shape((1024, D), low), shape((...  251 us
    pallas_call x2, Pallas kernels, update_plain(): pl.pallas_call(lambda *refs: update_kernel(first, slots, *refs), grid=(co...  14.8 us
    pallas_call x1, Pallas kernels, update_attention(): pl.pallas_call(update_attention_kernel, grid=(256 // block,), out_shape=(...  14.7 us

profile of v1, /device:TPU:16, one launch (start us, length us, event | category | flops | bytes accessed | tf_op | source)
XLA Modules:
  0.0 586.6 jit_solution(9957064566712963841)
XLA Ops:
  0.7 0.7 compare_select_fusion
  1.3 1.2 scatter_custom_fusion.order_ref
  2.5 1.5 reshape.101.par.gains_ref
  4.0 0.0 copy-start.9
  4.0 0.0 copy-start.13
  4.1 285.2 %shard_map.336 = (bf16[32,32,1024]{2,1,0:T(8,128)(2,1)}, bf16[16,4,256,1024]{3,2,1,0:T(8,128)(2,1)}, bf16[1024,1024]{1,0:T(8,128)(2,1)}, bf16[1024,1024]{1,0:T(8...) custom-call(s32[32]{0:T(128)} %scatter_custom_fusion.order_ref, ...), custom_call_target="tpu_custom_call" | custom-call | tf_op jit(solution)/shard_map/pallas_call | solution.py:902
  289.3 0.0 copy-done.12
  289.3 0.0 copy-done.11
  289.3 0.0 copy-done.15
  289.4 0.1 copy.50
  289.5 0.7 pad.4.rows_ref
  290.2 0.0 copy-done.10
  290.2 0.1 pad.8.clone
  290.3 0.0 copy-done.9
  290.3 0.0 copy-done.13
  290.3 0.7 maximum_maximum_fusion.cols_ref
  291.0 251.0 %shard_map.337 = (bf16[1024,1024]{1,0:T(8,128)(2,1)}, bf16[128,1024]{1,0:T(8,128)(2,1)}, bf16[16,256,1024]{2,1,0:T(8,128)(2,1)}, f32[24,1024]{1,0:T(8,128)}, f32...) custom-call(s32[32]{0:T(128)} %lengths_ref.3, ...), custom_call_target="tpu_custom_call" | custom-call | tf_op jit(solution)/shard_map/pallas_call | solution.py:1796
  542.0 0.0 copy-start
  542.0 14.7 %shard_map.338 = (f32[2048,1024]{1,0:T(8,128)}, f32[2048,1024]{1,0:T(8,128)}, bf16[2048,1024]{1,0:T(8,128)(2,1)}) custom-call(bf16[16,256,1024]{2,1,0:T(8,128)(2,1)} %get-tuple-element.84.grad_ref.refs_0_, f32[2048,1024]{1,0:T(8,128)} %bitcast.33, f32[256,128]{1,0:T(8,128)} %get-tuple-element.85.rows_ref, f32[16,1024]{1,0:T(8,128)} %get-tuple-element.86.scale_ref.refs_3_), custom_call_target="tpu_custom_call" | custom-call | tf_op jit(solution)/shard_map/pallas_call | solution.py:1893
  556.7 0.0 copy-done
  556.7 1.3 slice_reduce_fusion
  558.0 7.2 %shard_map.339 = (f32[256,4096]{1,0:T(8,128)}, f32[256,4096]{1,0:T(8,128)}, bf16[256,4096]{1,0:T(8,128)(2,1)}) custom-call(bf16[16,256,1024]{2,1,0:T(8,128)(2,1)} %get-tuple-element.84.grad_ref.refs_0_, f32[256,4096]{1,0:T(8,128)} %refs_1_.2, f32[256,1]{1,0:T(8,128)} %get-tuple-element.167.refs_2_, f32[16,1024]{1,0:T(8,128)} %get-tuple-element.86.scale_ref.refs_3_), custom_call_target="tpu_custom_call" | custom-call | tf_op jit(solution)/shard_map/pallas_call | solution.py:1937
  565.2 0.1 slice_bitcast_fusion.1
  565.3 0.1 copy.51
  565.4 1.0 copy.57
  566.5 0.0 copy-start.14
  566.5 7.5 %shard_map.340 = (f32[1024,1024]{1,0:T(8,128)}, f32[1024,1024]{1,0:T(8,128)}, bf16[1024,1024]{1,0:T(8,128)(2,1)}) custom-call(bf16[16,256,1024]{2,1,0:T(8,128)(2,1)} %get-tuple-element.84.grad_ref.refs_0_, f32[1024,1024]{1,0:T(8,128)} %refs_1_.3, f32[1024,1]{1,0:T(8,128)} %bitcast.37, f32[16,1024]{1,0:T(8,128)} %get-tuple-element.86.scale_ref.refs_3_), custom_call_target="tpu_custom_call" | custom-call | tf_op jit(solution)/shard_map/pallas_call | solution.py:1937
  574.0 0.0 copy-done.6
  574.1 0.0 copy-start.2
  574.1 0.0 copy-done.7
  574.1 0.6 multiply_reduce_fusion
  575.4 0.0 copy-done.3
  575.4 0.7 divide_subtract_fusion
  576.1 0.0 copy-start.1
  576.1 0.7 copy.55
  576.8 0.0 copy-done.8
  576.8 0.6 slice.29
  577.4 0.6 copy.58
  578.0 0.6 copy.59
  578.6 0.6 slice.31
  579.2 0.0 copy-done.14
  579.2 0.6 reduce_sum.19
  580.5 0.5 sqrt_bitcast_fusion
  581.0 3.1 copy.63
  584.1 0.0 copy-done.1
  584.1 1.3 copy.64
  585.5 0.0 copy-done.2
  585.5 0.7 copy.65
  (21 shorter events, 0.1 us)
Async XLA Ops:
  4.0 285.3 %copy-start.12 = (f32[1024]{0:T(1024)S(1)}, f32[1024]{0:T(1024)}, u32[]{:S(2)}) copy-start(f32[1024]{0:T(1024)} %param.31) | copy-start | bytes 12292
  4.0 285.3 %copy-start.11 = (f32[8,256]{1,0:T(8,128)S(1)}, f32[8,256]{1,0:T(8,128)}, u32[]{:S(2)}) copy-start(f32[8,256]{1,0:T(8,128)} %param.27) | copy-start | bytes 24580
  4.0 285.3 %copy-start.15 = (f32[256]{0:T(256)S(1)}, f32[256]{0:T(256)}, u32[]{:S(2)}) copy-start(f32[256]{0:T(256)} %param.29) | copy-start | bytes 3076
  4.0 286.1 %copy-start.10 = (f32[4096]{0:T(1024)S(1)}, f32[4096]{0:T(1024)}, u32[]{:S(2)}) copy-start(f32[4096]{0:T(1024)} %param.30) | copy-start | bytes 49156
  4.0 286.2 %copy-start.9 = (f32[8,1024]{1,0:T(8,128)S(1)}, f32[8,1024]{1,0:T(8,128)}, u32[]{:S(2)}) copy-start(f32[8,1024]{1,0:T(8,128)} %param.28) | copy-start | bytes 98308
  4.0 286.2 %copy-start.13 = (f32[1024]{0:T(1024)S(1)}, f32[1024]{0:T(1024)}, u32[]{:S(2)}) copy-start(f32[1024]{0:T(1024)} %param.32) | copy-start | bytes 12292
  542.0 14.7 %copy-start = (f32[256,128]{1,0:T(8,128)S(1)}, f32[256,128]{1,0:T(8,128)}, u32[]{:S(2)}) copy-start(f32[256,128]{1,0:T(8,128)} %get-tuple-element.85.rows_ref) | copy-start | bytes 393220
  566.5 7.6 %copy-start.6 = (f32[24,1024]{1,0:T(8,128)S(1)}, f32[24,1024]{1,0:T(8,128)}, u32[]{:S(2)}) copy-start(f32[24,1024]{1,0:T(8,128)} %get-tuple-element.90) | copy-start | bytes 294916
  566.5 7.6 %copy-start.7 = (f32[17408]{0:T(1024)S(1)}, f32[17408]{0:T(1024)}, u32[]{:S(2)}) copy-start(f32[17408]{0:T(1024)} %param.33) | copy-start | bytes 208900
  566.5 8.9 %copy-start.3 = (f32[17408]{0:T(1024)S(1)}, f32[17408]{0:T(1024)}, u32[]{:S(2)}) copy-start(f32[17408]{0:T(1024)} %param.26) | copy-start | bytes 208900
  566.5 10.3 %copy-start.8 = (f32[16,1024]{1,0:T(8,128)S(1)}, f32[16,1024]{1,0:T(8,128)}, u32[]{:S(2)}) copy-start(f32[16,1024]{1,0:T(8,128)} %get-tuple-element.97) | copy-start | bytes 196612
  566.5 12.7 %copy-start.14 = (s32[32]{0:T(128)S(1)}, s32[32]{0:T(128)}, u32[]{:S(2)}) copy-start(s32[32]{0:T(128)} %lengths_ref.3) | copy-start | bytes 388
  574.1 11.4 %copy-start.2 = (f32[17408]{0:T(1024)}, f32[17408]{0:T(1024)S(1)}, u32[]{:S(2)}) copy-start(f32[17408]{0:T(1024)S(1)} %reshape.111) | copy-start | bytes 208900
  574.7 10.8 %copy-start.4 = (f32[17408]{0:T(1024)}, f32[17408]{0:T(1024)S(1)}, u32[]{:S(2)}) copy-start(f32[17408]{0:T(1024)S(1)} %get-tuple-element.210) | copy-start | bytes 208900
  576.1 8.1 %copy-start.1 = (bf16[1024,1024]{1,0:T(8,128)(2,1)S(1)}, bf16[1024,1024]{1,0:T(8,128)(2,1)}, u32[]{:S(2)}) copy-start(bf16[1024,1024]{1,0:T(8,128)(2,1)} %get-tuple-element.191) | copy-start | bytes 6291460
  581.0 4.5 copy-start.5
